TPU v7x, 128 devices: a whole 4x4x4 slice. The times are simulated.
128 devices in a mesh: trow: 8 (over z, core), tcol: 16 (over x, y).
Axes of the slice: x: 4, y: 4, z: 4, core: 2. Of those that a mesh axis runs over, the one named last changes fastest.
Arguments:
- inputs: bfloat16 [2048, 8192], P('tcol', 'trow'), may hold values from -6 to 6
- grad_out: bfloat16 [2048, 8192], P('tcol', 'trow'), may hold values from -6 to 6
- pre_act: bfloat16 [2048, 16384], P('trow', 'tcol'), may hold values from -8 to 8
- up_w: bfloat16 [8, 64, 512, 512], P('trow', 'tcol'), may hold values from -0.0625 to 0.0625
- up_noise: bfloat16 [8, 64, 512, 512], P('trow', 'tcol'), may hold values from -0.3984375 to 0.3984375
- down_w: bfloat16 [8, 64, 512, 512], P('trow', 'tcol'), may hold values from -0.046875 to 0.046875
- down_noise: bfloat16 [8, 64, 512, 512], P('trow', 'tcol'), may hold values from -0.3984375 to 0.3984375
- up_slot: int32 [8, 64], P('trow', 'tcol'), may hold values from -1 to 3, as said below
- down_slot: int32 [8, 64], P('trow', 'tcol'), may hold values from -1 to 3, as said below
Outputs:
- input_grad: bfloat16 [2048, 8192], P('tcol', 'trow')
- up_grad: float32 [8, 64, 512, 512], P('trow', 'tcol')
- down_grad: float32 [8, 64, 512, 512], P('trow', 'tcol')
Inputs may be any that keep to these rules, and one draw needn't show every extreme that they name: Each device's 4 entries of up_slot name distinct local positions in rising order, followed by -1 for empty slots; every device keeps at least one tile, one device keeps all 4 and another exactly one. `down_slot`: as for up_slot, drawn independently.
All inputs are finite; a program needn't handle non-finite values.
Results may differ from a plain program's by a relative error of at most 0.033.
Values may be sent and summed in bfloat16 or wider, within the bound.
No kernel may reach another device: no remote copies, remote signals or barrier semaphores. Data moves between devices by JAX's collectives and lax.ppermute only.
A program may use at most 128 MiB of HBM per device.

v0:
```python
import functools

import jax
import jax.numpy as jnp
from jax import lax
from jax.experimental import pallas as pl
from jax.experimental.pallas import tpu as pltpu
from jax.sharding import Mesh, PartitionSpec as P


PLANE = ("c", "x", "y")
GRADS_VMEM = 24 * 2**20


def along(step, value, is_first):
    pairs = []
    for c in range(2):
        for x in range(4):
            for y in range(4):
                to = ((x + step) % 4, y) if (c == 0) == is_first else (x, (y + step) % 4)
                pairs.append(((c * 4 + x) * 4 + y, (c * 4 + to[0]) * 4 + to[1]))
    return lax.ppermute(value, PLANE, pairs)


def plane(step, value):
    return along(step, value, False)


def exchange_first(value):
    lines = [[x * 4 + y for x in range(4)] for y in range(4)]
    lines += [[16 + x * 4 + y for y in range(4)] for x in range(4)]
    return lax.all_to_all(value, PLANE, 0, 0, axis_index_groups=lines, tiled=True)


def exchange_z(value):
    return lax.all_to_all(value, "z", 0, 0, tiled=True)


def four(value):
    return jnp.broadcast_to(value[None], (4,) + value.shape)


def swap(value):
    return lax.ppermute(value, "c", [(0, 1), (1, 0)])


def unsigned(starts):
    return [jnp.uint32(i) if isinstance(i, int) else i for i in starts]


def put(buffer, value, starts):
    return lax.dynamic_update_slice(buffer, value, unsigned(starts))


def take(array, index, axis=0):
    starts = [0] * array.ndim
    starts[axis] = index
    sizes = list(array.shape)
    sizes[axis] = 1
    return lax.squeeze(lax.dynamic_slice(array, unsigned(starts), sizes), (axis,))


def after(value, *others):
    return lax.optimization_barrier((value, *others))[0]


def silu_slope(values):
    wide = values.astype(jnp.float32)
    sigma = jax.nn.sigmoid(wide)
    return sigma * (1.0 + wide * (1.0 - sigma))


def weights_kernel(slots, stored, noise, out):
    place = pl.program_id(0)
    live = slots[0] == place
    for s in range(1, 4):
        live = live | (slots[s] == place)

    @pl.when(live)
    def _():
        wide = stored[0].astype(jnp.float32) * (1.0 + noise[0].astype(jnp.float32))
        out[...] = wide.astype(out.dtype)

    @pl.when(jnp.logical_not(live))
    def _():
        out[...] = jnp.zeros_like(out)


def dense_weights(slots, stored, noise, hidden_rows):
    size = stored.shape[-1]

    def held_at(place, slots):
        index = jnp.int32(0)
        for s in range(1, 4):
            index = index + jnp.where(slots[s] == place, s, 0)
        return index, 0, 0

    def out_at(place, slots):
        return (place % 2, place // 2) if hidden_rows else (place // 2, place % 2)

    tile = pl.BlockSpec((1, size, size), held_at)
    return pl.pallas_call(
        weights_kernel,
        grid_spec=pltpu.PrefetchScalarGridSpec(
            num_scalar_prefetch=1,
            grid=(4,),
            in_specs=[tile, tile],
            out_specs=pl.BlockSpec((size, size), out_at),
        ),
        out_shape=jax.ShapeDtypeStruct((2 * size, 2 * size), stored.dtype),
        cost_estimate=pl.CostEstimate(flops=8 * size * size, bytes_accessed=24 * size * size, transcendentals=0),
        name="dense_weights",
    )(slots, stored, noise)


def grads_kernel(down, n_left, slots, place_of, *refs):
    lefts, owns, others = refs[:n_left], refs[n_left : n_left + 2], refs[n_left + 2 : -5]
    noise, out, left, right, sems = refs[-5:]
    s = pl.program_id(0)
    size, width, rows = out.shape[1], left.shape[-1], left.shape[-2]
    tk = others[0].shape[2]
    core, x, y = place_of[0], place_of[1], place_of[2]
    place = slots[s]
    hidden = pl.ds(pl.multiple_of((place & 1) * size, size), size)
    feature = pl.ds(pl.multiple_of((place >> 1) * size, size), size)
    a, b = (hidden, feature) if down else (feature, hidden)

    def line_at(array, half, from_core, d):
        return array.at[half, :, (y + d) & 3] if from_core == 0 else array.at[half, (x + d) & 3]

    def copies(me, half):
        pairs = []
        if down:
            for source, of in zip(lefts, (me, 1 - me)):
                pairs.append((source.at[:, :, half], left.at[half, :, pl.ds(2 * of, 2)]))
        else:
            for d, source in enumerate(lefts):
                pairs.append((source.at[:, half], line_at(left, half, me, d)))
        for k in range(2):
            for d in range(4):
                source = (owns if half == me else others)[k].at[d, :, :, pl.ds(0, width)]
                pairs.append((source, line_at(right, half, half, d).at[:, pl.ds(k * tk, tk)]))
        first = half * 12
        return [pltpu.make_async_copy(*pair, sems.at[first + i]) for i, pair in enumerate(pairs)]

    @pl.when(s == 0)
    def _():
        for me in range(2):

            @pl.when(core == me)
            def _():
                for half in range(2):
                    for copy in copies(me, half):
                        copy.start()

    for half in range(2):

        @pl.when(s == 0)
        def _():
            for me in range(2):

                @pl.when(core == me)
                def _():
                    for copy in copies(me, half):
                        copy.wait()

            if down:

                @pl.loop(0, 16)
                def _(i):
                    wide = left[half, i >> 2, i & 3].astype(jnp.float32)
                    left[half, i >> 2, i & 3] = (wide * jax.nn.sigmoid(wide)).astype(left.dtype)

        @pl.when(place >= 0)
        def _():
            rows_first = (((0,), (0,)), ((), ()))
            more = lax.dot_general(
                left[half, :, :, :, a].reshape(16 * rows, size),
                right[half, :, :, :, b].reshape(16 * rows, size),
                rows_first,
                preferred_element_type=jnp.float32,
            )
            if half == 0:
                out[0] = more
            else:
                out[0] = (more + out[0]) * (1.0 + noise[0].astype(jnp.float32))

    @pl.when(place < 0)
    def _():
        out[...] = jnp.zeros_like(out)


def slot_grads(slots, place_of, lefts, owns, others, noise, down):
    rows, width = lefts[0].shape[-2:]
    size = noise.shape[-1]
    tile = pl.BlockSpec((1, size, size), lambda s, *_: (s, 0, 0))
    anywhere = pl.BlockSpec(memory_space=pl.ANY)
    whole = pltpu.VMEM((2, 4, 4, rows, width), noise.dtype)
    return pl.pallas_call(
        functools.partial(grads_kernel, down, len(lefts)),
        grid_spec=pltpu.PrefetchScalarGridSpec(
            num_scalar_prefetch=2,
            grid=(4,),
            in_specs=[anywhere] * (len(lefts) + len(owns) + len(others)) + [tile],
            out_specs=tile,
            scratch_shapes=[whole, whole, pltpu.SemaphoreType.DMA((24,))],
        ),
        out_shape=jax.ShapeDtypeStruct(noise.shape, jnp.float32),
        compiler_params=pltpu.CompilerParams(vmem_limit_bytes=GRADS_VMEM),
        cost_estimate=pl.CostEstimate(
            flops=8 * 32 * rows * size * size, bytes_accessed=14 * 2**20, transcendentals=0
        ),
        name="slot_grads",
    )(slots, place_of, *lefts, *owns, *others, noise)


def dot(a, b, contract, kind):
    return lax.dot_general(a, b, (contract, ((), ())), preferred_element_type=jnp.float32).astype(kind)


def add_up(parts):
    total = parts[0].astype(jnp.float32)
    for part in parts[1:]:
        total = total + part.astype(jnp.float32)
    return total


def on_device(inputs, grad_out, pre_act, up_w, up_noise, down_w, down_noise, up_slot, down_slot):
    z, c, x, y = (lax.axis_index(a).astype(jnp.uint32) for a in ("z", "c", "x", "y"))
    first, second = jnp.where(c == 0, x, y), jnp.where(c == 0, y, x)
    other_c = c ^ jnp.uint32(1)
    ahead = lambda index, d: (index + jnp.asarray(d, jnp.uint32)) & jnp.uint32(3)
    bf16 = jnp.bfloat16
    rows, feats = grad_out.shape
    hidden = pre_act.shape[1]
    half = rows // 2
    tk = half // 2
    up_slots, down_slots = up_slot[0], down_slot[0]
    place_of = jnp.stack([c, x, y]).astype(jnp.int32)

    def down_product(dy):
        return dot(dy.reshape(-1, 2 * feats), down_both, ((1,), (1,)), bf16).reshape(4, -1, hidden)

    def up_product(hg):
        return dot(hg.reshape(-1, hidden), up_both, ((1,), (1,)), bf16).reshape(4, 4, tk, 2 * feats)

    def sum_of_four(parts):
        return add_up([parts[i] for i in range(4)])

    def pieces_of(line):
        return [plane(-d, line) for d in (1, 2, 3)]

    halves = grad_out.reshape(2, half, feats)
    here = jnp.concatenate([take(halves, c), swap(take(halves, other_c)), inputs], 0)
    down_own = dense_weights(down_slots, after(down_w, here)[0], down_noise[0], True)
    line = put(jnp.zeros((4,) + here.shape, bf16), here[None], (first, 0, 0))
    for d in (1, 3, 2):
        line = put(line, after(along(-d, here, True), down_own)[None], (ahead(first, d), 0, 0))

    h_own = exchange_z(four(pre_act)).reshape(4, 2, 2, half, hidden)
    line_a = jnp.concatenate([line[:, :tk], line[:, half : half + tk]], 2)
    line_b = jnp.concatenate([line[:, tk:half], line[:, half + tk : rows]], 2)
    line_x = line[:, rows:]
    down_both = jnp.concatenate([down_own, swap(down_own)], 1)

    pieces_a = [line_a, *pieces_of(line_a)]
    line_b, line_x = lax.optimization_barrier((line_b, line_x, *pieces_a))[:2]
    dy_a = jnp.stack(pieces_a)
    partial_a = down_product(after(dy_a, line_x))

    parts_a = exchange_z(after(partial_a, h_own))
    up_own = dense_weights(up_slots, after(up_w, partial_a)[0], up_noise[0], False)
    up_both = jnp.concatenate([up_own, swap(up_own)], 0)

    h_other = swap(h_own)
    at = ahead(second, z)
    near = at < jnp.uint32(2)
    on_0 = jnp.where(near, take(h_own, at & jnp.uint32(1), 1)[:, 0], take(h_other, at & jnp.uint32(1), 1)[:, 0])
    on_1 = jnp.concatenate([take(h_other, at)[:, 1], take(h_own, at)[:, 1]], 0)
    h_mine = jnp.where(c == 0, on_0, on_1)

    def hidden_grad(parts, k):
        slope = silu_slope(h_mine[:, k * tk : (k + 1) * tk].reshape(4 * tk, hidden))
        return (sum_of_four(parts) * slope).astype(bf16)

    hg_a = hidden_grad(after(parts_a, up_own), 0)
    other_a = swap(after(dy_a, partial_a)[..., feats:])
    dy_b = jnp.stack([line_b, *pieces_of(line_b)])
    partial_b = down_product(dy_b)
    all_a = after(exchange_z(four(hg_a)), partial_b, other_a)
    line_x = after(line_x, hg_a, dy_b)
    x_lines = [line_x, *pieces_of(line_x)]

    parts_b = exchange_z(after(partial_b, all_a))
    out_a = up_product(all_a)
    hg_b = hidden_grad(after(parts_b, out_a, *x_lines), 1)
    other_b = swap(after(dy_b, out_a)[..., feats:])
    own_a, *sent_a = lax.optimization_barrier([out_a[d] for d in range(4)])
    sum_a = add_up([own_a] + [plane(d, sent_a[d - 1]) for d in (1, 2, 3)]).astype(bf16)
    all_b = after(exchange_z(four(hg_b)), other_b, sum_a)
    out_b = up_product(all_b)
    own_b, *sent_b = lax.optimization_barrier([out_b[d] for d in range(4)])
    mine_a = sum_of_four(exchange_first(after(sum_a, all_b)))
    down_grad = slot_grads(
        down_slots, place_of, [h_own, h_other], [dy_a, dy_b], [other_a, other_b], down_noise[0], True
    )
    hgs = [hg.reshape(4, 4, tk, hidden) for hg in (all_a, all_b)]
    other_hgs = [swap(hg) for hg in hgs]
    sent_b = [after(plane(d, sent_b[d - 1]), down_grad, mine_a, *other_hgs) for d in (1, 2, 3)]
    sum_b = add_up([own_b] + sent_b).astype(bf16)
    x_lines = [line_x.reshape(4, 2, half, feats) for line_x in x_lines]
    up_grad = slot_grads(up_slots, place_of, x_lines, hgs, other_hgs, up_noise[0], False)
    mine_b = sum_of_four(after(exchange_first(sum_b), up_grad))
    mine = jnp.concatenate([mine_a, mine_b], 0).astype(bf16)
    input_grad = jnp.zeros((2, half, feats), bf16)
    input_grad = put(input_grad, mine[None, :, :feats], (c, 0, 0))
    input_grad = put(input_grad, swap(mine[:, feats:])[None], (other_c, 0, 0))
    return input_grad.reshape(rows, feats), up_grad[None], down_grad[None]


def solution(mesh):
    fine = Mesh(mesh.devices.reshape(4, 2, 4, 4), ("z", "c", "x", "y"))
    row, col = ("z", "c"), ("x", "y")
    in_specs = (P(col, row), P(col, row), P(row, col)) + (P(row, col),) * 6
    out_specs = (P(col, row), P(row, col), P(row, col))
    return jax.shard_map(
        on_device, mesh=fine, in_specs=in_specs, out_specs=out_specs, check_vma=False
    )
```

profile of v0, /device:TPU:1, one launch (start us, length us, event | category | flops | bytes accessed | tf_op | source)
XLA Modules:
  0.0 188.4 jit_solution(10073410417322971102)
XLA Ops:
  5.1 2.9 %collective-permute-start.1 = (bf16[256,1024]{1,0:T(8,128)(2,1)S(1)}, bf16[256,1024]{1,0:T(8,128)(2,1)S(1)}, u32[]{:S(2)}, u32[]{:S(2)}) collective-permute-start(bf16[256,1024]{1,0:T(8,128)(2,1)S(1)} %pad_maximum_fusion.12), channel_id=1, source_target_pairs={{0,12},{1,13},{2,14},{3,15},{4,0},{5,1},{6,2},{7,3},{8,4},{9,5},{1... | collective-permute-start | bytes 1572872 | tf_op jit(solution)/shard_map/ppermute | solution.py:22
  12.3 5.0 %all-to-all-start = ((bf16[4,256,1024]{2,1,0:T(8,128)(2,1)}), bf16[4,256,1024]{2,1,0:T(8,128)(2,1)S(1)}, u32[]{:S(2)}, u32[]{:S(2)}) async-start(bf16[4,256,1024]{2,1,0:T(8,128)(2,1)} %broadcast_in_dim.58), calls=%async_computation | async-start | bytes 4194304 | tf_op jit(solution)/shard_map/all_to_all | solution.py:36
  17.3 3.9 %dense_weights.2 = bf16[1024,1024]{1,0:T(8,128)(2,1)} custom-call(s32[4]{0:T(128)} %bitcast.116, bf16[4,512,512]{2,1,0:T(8,128)(2,1)} %bitcast.121, bf16[4,512,512]{2,1,0:T(8,128)(2,1)} %bitcast.112), custom_call_target="tpu_custom_call" | custom-call | flops 2097152 | bytes 6291456 | tf_op jit(solution)/shard_map/dense_weights/pallas_call | solution.py:102
  31.7 10.8 %all-to-all-done = bf16[4,256,1024]{2,1,0:T(8,128)(2,1)S(1)} async-done(((bf16[4,256,1024]{2,1,0:T(8,128)(2,1)}), bf16[4,256,1024]{2,1,0:T(8,128)(2,1)S(1)}, u32[]{:S(2)}, u32[]{:S(2)}) %all-to-all-start) | async-done | bytes 2097184 | tf_op jit(solution)/shard_map/all_to_all | solution.py:36
  49.7 5.4 %fusion.2 = bf16[512,1024]{1,0:T(8,128)(2,1)} fusion(bf16[512,2048]{1,0:T(8,128)(2,1)S(1)} %bitcast.110, bf16[1024,1024]{1,0:T(8,128)(2,1)} %collective-permute-done.7, bf16[1024,1024]{1,0:T(8,128)(2,1)S(1)} %copy-done.14), kind=kOutput, calls=%fused_computation.8 | convolution fusion | flops 2156396544 | bytes 7340032 | tf_op jit(solution)/shard_map/dot_general | solution.py:218
  55.2 3.5 %all-to-all-start.1 = ((bf16[4,128,1024]{2,1,0:T(8,128)(2,1)}), bf16[4,128,1024]{2,1,0:T(8,128)(2,1)S(1)}, u32[]{:S(2)}, u32[]{:S(2)}) async-start(bf16[4,128,1024]{2,1,0:T(8,128)(2,1)} %bitcast.127), calls=%async_computation.1 | async-start | bytes 2097152 | tf_op jit(solution)/shard_map/all_to_all | solution.py:36
  63.6 3.9 %dense_weights.3 = bf16[1024,1024]{1,0:T(8,128)(2,1)} custom-call(s32[4]{0:T(128)} %bitcast.118, bf16[4,512,512]{2,1,0:T(8,128)(2,1)} %bitcast.122, bf16[4,512,512]{2,1,0:T(8,128)(2,1)} %bitcast.114), custom_call_target="tpu_custom_call" | custom-call | flops 2097152 | bytes 6291456 | tf_op jit(solution)/shard_map/dense_weights/pallas_call | solution.py:102
  70.8 3.2 %all-to-all-done.1 = bf16[4,128,1024]{2,1,0:T(8,128)(2,1)S(1)} async-done(((bf16[4,128,1024]{2,1,0:T(8,128)(2,1)}), bf16[4,128,1024]{2,1,0:T(8,128)(2,1)S(1)}, u32[]{:S(2)}, u32[]{:S(2)}) %all-to-all-start.1) | async-done | bytes 1048608 | tf_op jit(solution)/shard_map/all_to_all | solution.py:36
  80.8 4.2 %all-to-all-start.2 = ((bf16[4,128,1024]{2,1,0:T(8,128)(2,1)}), bf16[4,128,1024]{2,1,0:T(8,128)(2,1)}, u32[]{:S(2)}, u32[]{:S(2)}) async-start(bf16[4,128,1024]{2,1,0:T(8,128)(2,1)} %broadcast_in_dim.60), calls=%async_computation.2 | async-start | bytes 2097152 | tf_op jit(solution)/shard_map/all_to_all | solution.py:36
  90.7 4.9 %fusion.3 = bf16[512,1024]{1,0:T(8,128)(2,1)} fusion(bf16[512,2048]{1,0:T(8,128)(2,1)S(1)} %bitcast.111, bf16[1024,1024]{1,0:T(8,128)(2,1)} %collective-permute-done.7, bf16[1024,1024]{1,0:T(8,128)(2,1)S(1)} %copy-done.15), kind=kOutput, calls=%fused_computation.9 | convolution fusion | flops 2156396544 | bytes 7340032 | tf_op jit(solution)/shard_map/dot_general | solution.py:218
  95.7 4.7 %all-to-all-done.2 = bf16[4,128,1024]{2,1,0:T(8,128)(2,1)} async-done(((bf16[4,128,1024]{2,1,0:T(8,128)(2,1)}), bf16[4,128,1024]{2,1,0:T(8,128)(2,1)}, u32[]{:S(2)}, u32[]{:S(2)}) %all-to-all-start.2) | async-done | bytes 1048608 | tf_op jit(solution)/shard_map/all_to_all | solution.py:36
  100.4 4.3 %all-to-all-start.3 = ((bf16[4,128,1024]{2,1,0:T(8,128)(2,1)}), bf16[4,128,1024]{2,1,0:T(8,128)(2,1)}, u32[]{:S(2)}, u32[]{:S(2)}) async-start(bf16[4,128,1024]{2,1,0:T(8,128)(2,1)} %bitcast.126), calls=%async_computation.3 | async-start | bytes 2097152 | tf_op jit(solution)/shard_map/all_to_all | solution.py:36
  104.6 5.1 %convolution_convert_fusion.1 = bf16[512,2048]{1,0:T(8,128)(2,1)S(1)} fusion(bf16[512,1024]{1,0:T(8,128)(2,1)} %bitcast.36, bf16[1024,1024]{1,0:T(8,128)(2,1)} %collective-permute-done.13, bf16[1024,1024]{1,0:T(8,128)(2,1)} %dense_weights.3), kind=kOutput, calls=%fused_computation.3 | convolution fusion | flops 2156920832 | bytes 7340032 | tf_op jit(solution)/shard_map/dot_general | solution.py:218
  121.6 4.3 %all-to-all-start.4 = ((bf16[4,128,1024]{2,1,0:T(8,128)(2,1)}), bf16[4,128,1024]{2,1,0:T(8,128)(2,1)}, u32[]{:S(2)}, u32[]{:S(2)}) async-start(bf16[4,128,1024]{2,1,0:T(8,128)(2,1)} %broadcast_in_dim.62), calls=%async_computation.4 | async-start | bytes 2097152 | tf_op jit(solution)/shard_map/all_to_all | solution.py:36
  127.7 3.4 %collective-permute-done.14 = bf16[4,32,2048]{2,1,0:T(8,128)(2,1)} collective-permute-done((bf16[4,32,2048]{2,1,0:T(8,128)(2,1)}, bf16[4,32,2048]{2,1,0:T(8,128)(2,1)}, u32[]{:S(2)}, u32[]{:S(2)}) %collective-permute-start.14) | collective-permute-done | bytes 524320 | tf_op jit(solution)/shard_map/ppermute | solution.py:22
  133.7 5.5 %all-to-all-done.4 = bf16[4,128,1024]{2,1,0:T(8,128)(2,1)} async-done(((bf16[4,128,1024]{2,1,0:T(8,128)(2,1)}), bf16[4,128,1024]{2,1,0:T(8,128)(2,1)}, u32[]{:S(2)}, u32[]{:S(2)}) %all-to-all-start.4) | async-done | bytes 1048608 | tf_op jit(solution)/shard_map/all_to_all | solution.py:36
  139.2 4.1 %all-to-all-start.5 = ((bf16[4,32,2048]{2,1,0:T(8,128)(2,1)}), bf16[4,32,2048]{2,1,0:T(8,128)(2,1)}, u32[]{:S(2)}, u32[]{:S(2)}) async-start(bf16[4,32,2048]{2,1,0:T(8,128)(2,1)} %add_convert_fusion.1), calls=%async_computation.5 | async-start | bytes 1048576 | tf_op jit(solution)/shard_map/all_to_all | solution.py:32
  143.4 2.8 %collective-permute-start.23 = (bf16[4,4,32,1024]{3,2,1,0:T(8,128)(2,1)}, bf16[4,4,32,1024]{3,2,1,0:T(8,128)(2,1)}, u32[]{:S(2)}, u32[]{:S(2)}) collective-permute-start(bf16[4,4,32,1024]{3,2,1,0:T(8,128)(2,1)} %bitcast.55.refs_5_), channel_id=1, source_target_pairs={{0,16},{16,0},{1,17},{17,1},{2,18},{18,2},{3,19},{19,3},{4,20},{20... | collective-permute-start | bytes 3145736 | tf_op jit(solution)/shard_map/ppermute | solution.py:44
  146.2 5.1 %convolution_convert_fusion = bf16[512,2048]{1,0:T(8,128)(2,1)S(1)} fusion(bf16[512,1024]{1,0:T(8,128)(2,1)} %bitcast.46, bf16[1024,1024]{1,0:T(8,128)(2,1)} %collective-permute-done.13, bf16[1024,1024]{1,0:T(8,128)(2,1)} %dense_weights.3), kind=kOutput, calls=%fused_computation.2 | convolution fusion | flops 2156920832 | bytes 7340032 | tf_op jit(solution)/shard_map/dot_general | solution.py:218
  152.7 3.0 %collective-permute-start.25 = (bf16[4,32,2048]{2,1,0:T(8,128)(2,1)}, bf16[4,32,2048]{2,1,0:T(8,128)(2,1)}, u32[]{:S(2)}, u32[]{:S(2)}) collective-permute-start(bf16[4,32,2048]{2,1,0:T(8,128)(2,1)} %bitcast.50), channel_id=1, source_target_pairs={{0,3},{1,0},{2,1},{3,2},{4,7},{5,4},{6,5},{7,6},{8,11},{9,8},{10,9... | collective-permute-start | bytes 1572872 | tf_op jit(solution)/shard_map/ppermute | solution.py:22
  156.8 7.8 %slot_grads.2 = f32[4,512,512]{2,1,0:T(8,128)} custom-call(s32[4]{0:T(128)S(1)} %bitcast.117, s32[3]{0:T(128)S(1)} %add_convert_fusion.3.place_of, bf16[4,2,2,64,1024]{4,3,2,1,0:T(8,128)(2,1)S(1)} %bitcast.109, bf16[4,2,2,64,1024]{4,3,2,1,0:T(8,128)(2,1)} %collective-permute-done.8.refs_1_, bf16[4,4,32,2048]{3,2,1,0:T(8,128)(2,1)S(1)} %copy-done.2, ...), custom_call_target="tpu_custom_call" | custom-call | flops 4294967296 | bytes 14680064 | tf_op jit(solution)/shard_map/slot_grads/pallas_call | solution.py:199
  167.7 3.4 %collective-permute-done.21 = bf16[4,32,2048]{2,1,0:T(8,128)(2,1)} collective-permute-done((bf16[4,32,2048]{2,1,0:T(8,128)(2,1)}, bf16[4,32,2048]{2,1,0:T(8,128)(2,1)}, u32[]{:S(2)}, u32[]{:S(2)}) %collective-permute-start.21) | collective-permute-done | bytes 524320 | tf_op jit(solution)/shard_map/ppermute | solution.py:22
  173.7 3.5 %all-to-all-start.6 = ((bf16[4,32,2048]{2,1,0:T(8,128)(2,1)}), bf16[4,32,2048]{2,1,0:T(8,128)(2,1)S(1)}, u32[]{:S(2)}, u32[]{:S(2)}) async-start(bf16[4,32,2048]{2,1,0:T(8,128)(2,1)} %add_convert_fusion), calls=%async_computation.6 | async-start | bytes 1048576 | tf_op jit(solution)/shard_map/all_to_all | solution.py:32
  177.2 7.3 %slot_grads.3 = f32[4,512,512]{2,1,0:T(8,128)} custom-call(s32[4]{0:T(128)S(1)} %bitcast.119, s32[3]{0:T(128)S(1)} %add_convert_fusion.3.place_of, bf16[4,2,64,1024]{3,2,1,0:T(8,128)(2,1)} %bitcast.56.refs_0_, bf16[4,2,64,1024]{3,2,1,0:T(8,128)(2,1)} %bitcast.57.refs_1_, bf16[4,2,64,1024]{3,2,1,0:T(8,128)(2,1)} %bitcast.58.refs_2_, ...), custom_call_target="tpu_custom_call" | custom-call | flops 4294967296 | bytes 14680064 | tf_op jit(solution)/shard_map/slot_grads/pallas_call | solution.py:199
  (127 shorter events, 75.6 us)
Async XLA Ops:
  5.1 19.0 %collective-permute-start.1 = (bf16[256,1024]{1,0:T(8,128)(2,1)S(1)}, bf16[256,1024]{1,0:T(8,128)(2,1)S(1)}, u32[]{:S(2)}, u32[]{:S(2)}) collective-permute-start(bf16[256,1024]{1,0:T(8,128)(2,1)S(1)} %pad_maximum_fusion.12), channel_id=1, source_target_pairs={{0,12},{1,13},{2,14},{3,15},{4,0},{5,1},{6,2},{7,3},{8,4},{9,5},{1... | collective-permute-start | bytes 1572872 | tf_op jit(solution)/shard_map/ppermute | solution.py:22
  8.0 16.1 %collective-permute-start.3 = (bf16[256,1024]{1,0:T(8,128)(2,1)S(1)}, bf16[256,1024]{1,0:T(8,128)(2,1)}, u32[]{:S(2)}, u32[]{:S(2)}) collective-permute-start(bf16[256,1024]{1,0:T(8,128)(2,1)S(1)} %pad_maximum_fusion.12), channel_id=1, source_target_pairs={{0,8},{1,9},{2,10},{3,11},{4,12},{5,13},{6,14},{7,15},{8,0},{9,1},... | collective-permute-start | bytes 1572872 | tf_op jit(solution)/shard_map/ppermute | solution.py:22
  12.3 30.2 %all-to-all-start = ((bf16[4,256,1024]{2,1,0:T(8,128)(2,1)}), bf16[4,256,1024]{2,1,0:T(8,128)(2,1)S(1)}, u32[]{:S(2)}, u32[]{:S(2)}) async-start(bf16[4,256,1024]{2,1,0:T(8,128)(2,1)} %broadcast_in_dim.58), calls=%async_computation | async-start | bytes 4194304 | tf_op jit(solution)/shard_map/all_to_all | solution.py:36
  21.1 28.3 %collective-permute-start.7 = (bf16[1024,1024]{1,0:T(8,128)(2,1)}, bf16[1024,1024]{1,0:T(8,128)(2,1)}, u32[]{:S(2)}, u32[]{:S(2)}) collective-permute-start(bf16[1024,1024]{1,0:T(8,128)(2,1)} %dense_weights.2), channel_id=1, source_target_pairs={{0,16},{16,0},{1,17},{17,1},{2,18},{18,2},{3,19},{19,3},{4,20},{20... | collective-permute-start | bytes 6291464 | tf_op jit(solution)/shard_map/ppermute | solution.py:44
  27.6 20.1 %collective-permute-start.6 = (bf16[4,32,2048]{2,1,0:T(8,128)(2,1)}, bf16[4,32,2048]{2,1,0:T(8,128)(2,1)}, u32[]{:S(2)}, u32[]{:S(2)}) collective-permute-start(bf16[4,32,2048]{2,1,0:T(8,128)(2,1)} %get-tuple-element.78), channel_id=1, source_target_pairs={{0,1},{1,2},{2,3},{3,0},{4,5},{5,6},{6,7},{7,4},{8,9},{9,10},{10,1... | collective-permute-start | bytes 1572872 | tf_op jit(solution)/shard_map/ppermute | solution.py:22
  28.1 19.6 %collective-permute-start.5 = (bf16[4,32,2048]{2,1,0:T(8,128)(2,1)}, bf16[4,32,2048]{2,1,0:T(8,128)(2,1)}, u32[]{:S(2)}, u32[]{:S(2)}) collective-permute-start(bf16[4,32,2048]{2,1,0:T(8,128)(2,1)} %get-tuple-element.78), channel_id=1, source_target_pairs={{0,2},{1,3},{2,0},{3,1},{4,6},{5,7},{6,4},{7,5},{8,10},{9,11},{10,... | collective-permute-start | bytes 1572872 | tf_op jit(solution)/shard_map/ppermute | solution.py:22
  30.3 17.4 %collective-permute-start.4 = (bf16[4,32,2048]{2,1,0:T(8,128)(2,1)}, bf16[4,32,2048]{2,1,0:T(8,128)(2,1)}, u32[]{:S(2)}, u32[]{:S(2)}) collective-permute-start(bf16[4,32,2048]{2,1,0:T(8,128)(2,1)} %get-tuple-element.78), channel_id=1, source_target_pairs={{0,3},{1,0},{2,1},{3,2},{4,7},{5,4},{6,5},{7,6},{8,11},{9,8},{10,9... | collective-permute-start | bytes 1572872 | tf_op jit(solution)/shard_map/ppermute | solution.py:22
  42.4 32.6 %collective-permute-start.8 = (bf16[4,2,2,64,1024]{4,3,2,1,0:T(8,128)(2,1)S(1)}, bf16[4,2,2,64,1024]{4,3,2,1,0:T(8,128)(2,1)}, u32[]{:S(2)}, u32[]{:S(2)}) collective-permute-start(bf16[4,2,2,64,1024]{4,3,2,1,0:T(8,128)(2,1)S(1)} %bitcast.106), channel_id=1, source_target_pairs={{0,16},{16,0},{1,17},{17,1},{2,18},{18,2},{3,19},{19,3},{4,20},{20... | collective-permute-start | bytes 6291464 | tf_op jit(solution)/shard_map/ppermute | solution.py:44
  55.2 18.9 %all-to-all-start.1 = ((bf16[4,128,1024]{2,1,0:T(8,128)(2,1)}), bf16[4,128,1024]{2,1,0:T(8,128)(2,1)S(1)}, u32[]{:S(2)}, u32[]{:S(2)}) async-start(bf16[4,128,1024]{2,1,0:T(8,128)(2,1)} %bitcast.127), calls=%async_computation.1 | async-start | bytes 2097152 | tf_op jit(solution)/shard_map/all_to_all | solution.py:36
  58.7 26.4 %collective-permute-start.11 = (bf16[4,32,2048]{2,1,0:T(8,128)(2,1)}, bf16[4,32,2048]{2,1,0:T(8,128)(2,1)}, u32[]{:S(2)}, u32[]{:S(2)}) collective-permute-start(bf16[4,32,2048]{2,1,0:T(8,128)(2,1)} %pad_maximum_fusion.14), channel_id=1, source_target_pairs={{0,1},{1,2},{2,3},{3,0},{4,5},{5,6},{6,7},{7,4},{8,9},{9,10},{10,1... | collective-permute-start | bytes 1572872 | tf_op jit(solution)/shard_map/ppermute | solution.py:22
  60.0 25.1 %collective-permute-start.10 = (bf16[4,32,2048]{2,1,0:T(8,128)(2,1)}, bf16[4,32,2048]{2,1,0:T(8,128)(2,1)}, u32[]{:S(2)}, u32[]{:S(2)}) collective-permute-start(bf16[4,32,2048]{2,1,0:T(8,128)(2,1)} %pad_maximum_fusion.14), channel_id=1, source_target_pairs={{0,2},{1,3},{2,0},{3,1},{4,6},{5,7},{6,4},{7,5},{8,10},{9,11},{10,... | collective-permute-start | bytes 1572872 | tf_op jit(solution)/shard_map/ppermute | solution.py:22
  62.4 22.7 %collective-permute-start.9 = (bf16[4,32,2048]{2,1,0:T(8,128)(2,1)}, bf16[4,32,2048]{2,1,0:T(8,128)(2,1)}, u32[]{:S(2)}, u32[]{:S(2)}) collective-permute-start(bf16[4,32,2048]{2,1,0:T(8,128)(2,1)} %pad_maximum_fusion.14), channel_id=1, source_target_pairs={{0,3},{1,0},{2,1},{3,2},{4,7},{5,4},{6,5},{7,6},{8,11},{9,8},{10,9... | collective-permute-start | bytes 1572872 | tf_op jit(solution)/shard_map/ppermute | solution.py:22
  67.5 37.1 %collective-permute-start.13 = (bf16[1024,1024]{1,0:T(8,128)(2,1)}, bf16[1024,1024]{1,0:T(8,128)(2,1)}, u32[]{:S(2)}, u32[]{:S(2)}) collective-permute-start(bf16[1024,1024]{1,0:T(8,128)(2,1)} %dense_weights.3), channel_id=1, source_target_pairs={{0,16},{16,0},{1,17},{17,1},{2,18},{18,2},{3,19},{19,3},{4,20},{20... | collective-permute-start | bytes 6291464 | tf_op jit(solution)/shard_map/ppermute | solution.py:44
  75.0 20.7 %collective-permute-start.12 = (bf16[4,4,32,1024]{3,2,1,0:T(8,128)(2,1)}, bf16[4,4,32,1024]{3,2,1,0:T(8,128)(2,1)S(1)}, u32[]{:S(2)}, u32[]{:S(2)}) collective-permute-start(bf16[4,4,32,1024]{3,2,1,0:T(8,128)(2,1)} %slice.139), channel_id=1, source_target_pairs={{0,16},{16,0},{1,17},{17,1},{2,18},{18,2},{3,19},{19,3},{4,20},{20... | collective-permute-start | bytes 3145736 | tf_op jit(solution)/shard_map/ppermute | solution.py:44
  80.8 19.5 %all-to-all-start.2 = ((bf16[4,128,1024]{2,1,0:T(8,128)(2,1)}), bf16[4,128,1024]{2,1,0:T(8,128)(2,1)}, u32[]{:S(2)}, u32[]{:S(2)}) async-start(bf16[4,128,1024]{2,1,0:T(8,128)(2,1)} %broadcast_in_dim.60), calls=%async_computation.2 | async-start | bytes 2097152 | tf_op jit(solution)/shard_map/all_to_all | solution.py:36
  87.1 28.5 %collective-permute-start.17 = (bf16[4,128,1024]{2,1,0:T(8,128)(2,1)}, bf16[4,128,1024]{2,1,0:T(8,128)(2,1)}, u32[]{:S(2)}, u32[]{:S(2)}) collective-permute-start(bf16[4,128,1024]{2,1,0:T(8,128)(2,1)} %slice.168), channel_id=1, source_target_pairs={{0,3},{1,0},{2,1},{3,2},{4,7},{5,4},{6,5},{7,6},{8,11},{9,8},{10,9... | collective-permute-start | bytes 3145736 | tf_op jit(solution)/shard_map/ppermute | solution.py:22
  89.6 26.5 %collective-permute-start.18 = (bf16[4,128,1024]{2,1,0:T(8,128)(2,1)}, bf16[4,128,1024]{2,1,0:T(8,128)(2,1)}, u32[]{:S(2)}, u32[]{:S(2)}) collective-permute-start(bf16[4,128,1024]{2,1,0:T(8,128)(2,1)} %slice.168), channel_id=1, source_target_pairs={{0,2},{1,3},{2,0},{3,1},{4,6},{5,7},{6,4},{7,5},{8,10},{9,11},{10,... | collective-permute-start | bytes 3145736 | tf_op jit(solution)/shard_map/ppermute | solution.py:22
  90.2 26.8 %collective-permute-start.19 = (bf16[4,128,1024]{2,1,0:T(8,128)(2,1)}, bf16[4,128,1024]{2,1,0:T(8,128)(2,1)}, u32[]{:S(2)}, u32[]{:S(2)}) collective-permute-start(bf16[4,128,1024]{2,1,0:T(8,128)(2,1)} %slice.168), channel_id=1, source_target_pairs={{0,1},{1,2},{2,3},{3,0},{4,5},{5,6},{6,7},{7,4},{8,9},{9,10},{10,1... | collective-permute-start | bytes 3145736 | tf_op jit(solution)/shard_map/ppermute | solution.py:22
  100.4 18.6 %all-to-all-start.3 = ((bf16[4,128,1024]{2,1,0:T(8,128)(2,1)}), bf16[4,128,1024]{2,1,0:T(8,128)(2,1)}, u32[]{:S(2)}, u32[]{:S(2)}) async-start(bf16[4,128,1024]{2,1,0:T(8,128)(2,1)} %bitcast.126), calls=%async_computation.3 | async-start | bytes 2097152 | tf_op jit(solution)/shard_map/all_to_all | solution.py:36
  110.8 22.9 %collective-permute-start.20 = (bf16[4,4,32,1024]{3,2,1,0:T(8,128)(2,1)}, bf16[4,4,32,1024]{3,2,1,0:T(8,128)(2,1)}, u32[]{:S(2)}, u32[]{:S(2)}) collective-permute-start(bf16[4,4,32,1024]{3,2,1,0:T(8,128)(2,1)} %slice.149), channel_id=1, source_target_pairs={{0,16},{16,0},{1,17},{17,1},{2,18},{18,2},{3,19},{19,3},{4,20},{20... | collective-permute-start | bytes 3145736 | tf_op jit(solution)/shard_map/ppermute | solution.py:44
  121.6 17.7 %all-to-all-start.4 = ((bf16[4,128,1024]{2,1,0:T(8,128)(2,1)}), bf16[4,128,1024]{2,1,0:T(8,128)(2,1)}, u32[]{:S(2)}, u32[]{:S(2)}) async-start(bf16[4,128,1024]{2,1,0:T(8,128)(2,1)} %broadcast_in_dim.62), calls=%async_computation.4 | async-start | bytes 2097152 | tf_op jit(solution)/shard_map/all_to_all | solution.py:36
  125.9 40.0 %collective-permute-start.22 = (bf16[4,4,32,1024]{3,2,1,0:T(8,128)(2,1)}, bf16[4,4,32,1024]{3,2,1,0:T(8,128)(2,1)}, u32[]{:S(2)}, u32[]{:S(2)}) collective-permute-start(bf16[4,4,32,1024]{3,2,1,0:T(8,128)(2,1)} %bitcast.54.refs_4_), channel_id=1, source_target_pairs={{0,16},{16,0},{1,17},{17,1},{2,18},{18,2},{3,19},{19,3},{4,20},{20... | collective-permute-start | bytes 3145736 | tf_op jit(solution)/shard_map/ppermute | solution.py:44
  139.2 25.3 %all-to-all-start.5 = ((bf16[4,32,2048]{2,1,0:T(8,128)(2,1)}), bf16[4,32,2048]{2,1,0:T(8,128)(2,1)}, u32[]{:S(2)}, u32[]{:S(2)}) async-start(bf16[4,32,2048]{2,1,0:T(8,128)(2,1)} %add_convert_fusion.1), calls=%async_computation.5 | async-start | bytes 1048576 | tf_op jit(solution)/shard_map/all_to_all | solution.py:32
  143.4 24.3 %collective-permute-start.23 = (bf16[4,4,32,1024]{3,2,1,0:T(8,128)(2,1)}, bf16[4,4,32,1024]{3,2,1,0:T(8,128)(2,1)}, u32[]{:S(2)}, u32[]{:S(2)}) collective-permute-start(bf16[4,4,32,1024]{3,2,1,0:T(8,128)(2,1)} %bitcast.55.refs_5_), channel_id=1, source_target_pairs={{0,16},{16,0},{1,17},{17,1},{2,18},{18,2},{3,19},{19,3},{4,20},{20... | collective-permute-start | bytes 3145736 | tf_op jit(solution)/shard_map/ppermute | solution.py:44
  (28 other events, 210.7 us)
where the time goes:
time: 191 us; the launch traced here: 188 us
  starting transfers between devices  69.6 us (36%)
  waiting for transfers between devices  36.7 us (19%)
  Pallas kernels  22.7 us (12%)
  local copies, waits for them, and re-layouts  22.4 us (12%)
  matrix products  20.5 us (11%)
  other arithmetic  15.4 us (8%)
    all_to_all x5, waiting for transfers between devices, exchange_z(): return lax.all_to_all(value, 'z', 0, 0, tiled=True)  26.2 us
    ppermute x18, starting transfers between devices, along(): return lax.ppermute(value, PLANE, pairs)  25 us
    all_to_all x5, starting transfers between devices, exchange_z(): return lax.all_to_all(value, 'z', 0, 0, tiled=True)  21.3 us
    dot_general x4, matrix products, dot(): lax.dot_general(a, b, (contract, ((), ())), preferred_element_type=jnp.fl...  20.5 us
    ppermute x9, starting transfers between devices, swap(): return lax.ppermute(value, 'c', [(0, 1), (1, 0)])  15.6 us
    pallas_call x2, Pallas kernels, slot_grads(): pl.pallas_call(functools.partial(grads_kernel, down, len(lefts)), grid_sp...  15 us
    ppermute x18, waiting for transfers between devices, along(): return lax.ppermute(value, PLANE, pairs)  8.57 us
    pallas_call x2, Pallas kernels, dense_weights(): pl.pallas_call(weights_kernel, grid_spec=pltpu.PrefetchScalarGridSpec(num...  7.71 us
  transfers between devices with their start and end apart: 34, of which 10 were waited for; matrix products, arithmetic and copies ran while one was open for 27% of the time, Pallas kernels for 12%

commit v1 on v0

--- a/solution.py
+++ b/solution.py
@@ -9,7 +9,7 @@
 
 
 PLANE = ("c", "x", "y")
-GRADS_VMEM = 24 * 2**20
+GRADS_VMEM = 46 * 2**20
 
 
 def along(step, value, is_first):
@@ -113,12 +113,12 @@
     )(slots, stored, noise)
 
 
-def grads_kernel(down, n_left, slots, place_of, *refs):
-    lefts, owns, others = refs[:n_left], refs[n_left : n_left + 2], refs[n_left + 2 : -5]
+def grads_kernel(down, n_left, n_own, slots, place_of, *refs):
+    lefts, owns, others = refs[:n_left], refs[n_left : n_left + n_own], refs[n_left + n_own : -5]
     noise, out, left, right, sems = refs[-5:]
     s = pl.program_id(0)
     size, width, rows = out.shape[1], left.shape[-1], left.shape[-2]
-    tk = others[0].shape[2]
+    tk = others[0].shape[-2]
     core, x, y = place_of[0], place_of[1], place_of[2]
     place = slots[s]
     hidden = pl.ds(pl.multiple_of((place & 1) * size, size), size)
@@ -138,7 +138,10 @@
                 pairs.append((source.at[:, half], line_at(left, half, me, d)))
         for k in range(2):
             for d in range(4):
-                source = (owns if half == me else others)[k].at[d, :, :, pl.ds(0, width)]
+                if half == me:
+                    source = owns[4 * k + d].at[:, :, pl.ds(0, width)] if down else owns[k].at[d]
+                else:
+                    source = others[0].at[k, d] if len(others) == 1 else others[k].at[d]
                 pairs.append((source, line_at(right, half, half, d).at[:, pl.ds(k * tk, tk)]))
         first = half * 12
         return [pltpu.make_async_copy(*pair, sems.at[first + i]) for i, pair in enumerate(pairs)]
@@ -197,7 +200,7 @@
     anywhere = pl.BlockSpec(memory_space=pl.ANY)
     whole = pltpu.VMEM((2, 4, 4, rows, width), noise.dtype)
     return pl.pallas_call(
-        functools.partial(grads_kernel, down, len(lefts)),
+        functools.partial(grads_kernel, down, len(lefts), len(owns)),
         grid_spec=pltpu.PrefetchScalarGridSpec(
             num_scalar_prefetch=2,
             grid=(4,),
@@ -250,68 +253,79 @@
     def pieces_of(line):
         return [plane(-d, line) for d in (1, 2, 3)]
 
-    halves = grad_out.reshape(2, half, feats)
-    here = jnp.concatenate([take(halves, c), swap(take(halves, other_c)), inputs], 0)
+    def line_of(pieces):
+        line = jnp.zeros((4,) + pieces[0].shape, bf16)
+        for d, piece in enumerate(pieces):
+            line = put(line, piece[None], (ahead(first, d), 0, 0))
+        return line
+
+    halves, other_halves = (rows_of.reshape(2, half, feats) for rows_of in (grad_out, swap(grad_out)))
+    here = jnp.concatenate([take(halves, c), take(other_halves, c), inputs], 0)
     down_own = dense_weights(down_slots, after(down_w, here)[0], down_noise[0], True)
-    line = put(jnp.zeros((4,) + here.shape, bf16), here[None], (first, 0, 0))
-    for d in (1, 3, 2):
-        line = put(line, after(along(-d, here, True), down_own)[None], (ahead(first, d), 0, 0))
-
-    h_own = exchange_z(four(pre_act)).reshape(4, 2, 2, half, hidden)
-    line_a = jnp.concatenate([line[:, :tk], line[:, half : half + tk]], 2)
-    line_b = jnp.concatenate([line[:, tk:half], line[:, half + tk : rows]], 2)
-    line_x = line[:, rows:]
+    near = [here] + [after(along(-d, here, True), down_own) for d in (1, 2, 3)]
+    both = lambda piece, cut: jnp.concatenate([piece[:half][cut], piece[half:rows][cut]], 1)
+    line_a = line_of([both(piece, slice(0, tk)) for piece in near])
+    line_b = line_of([both(piece, slice(tk, half)) for piece in near])
+    line_x = line_of([after(piece, line_a)[rows:] for piece in near])
+
+    h_own = exchange_z(four(after(pre_act, here))).reshape(4, 2, 2, half, hidden)
     down_both = jnp.concatenate([down_own, swap(down_own)], 1)
 
+    up_own = dense_weights(up_slots, after(up_w, line_a)[0], up_noise[0], False)
     pieces_a = [line_a, *pieces_of(line_a)]
-    line_b, line_x = lax.optimization_barrier((line_b, line_x, *pieces_a))[:2]
     dy_a = jnp.stack(pieces_a)
-    partial_a = down_product(after(dy_a, line_x))
+    partial_a = down_product(after(dy_a, line_x, up_own))
 
     parts_a = exchange_z(after(partial_a, h_own))
-    up_own = dense_weights(up_slots, after(up_w, partial_a)[0], up_noise[0], False)
     up_both = jnp.concatenate([up_own, swap(up_own)], 0)
 
-    h_other = swap(h_own)
+    h_other = swap(after(h_own, partial_a))
+    h_here = after(h_own, h_other)
     at = ahead(second, z)
     near = at < jnp.uint32(2)
-    on_0 = jnp.where(near, take(h_own, at & jnp.uint32(1), 1)[:, 0], take(h_other, at & jnp.uint32(1), 1)[:, 0])
-    on_1 = jnp.concatenate([take(h_other, at)[:, 1], take(h_own, at)[:, 1]], 0)
+    on_0 = jnp.where(near, take(h_here, at & jnp.uint32(1), 1)[:, 0], take(h_other, at & jnp.uint32(1), 1)[:, 0])
+    on_1 = jnp.concatenate([take(h_other, at)[:, 1], take(h_here, at)[:, 1]], 0)
     h_mine = jnp.where(c == 0, on_0, on_1)
 
     def hidden_grad(parts, k):
-        slope = silu_slope(h_mine[:, k * tk : (k + 1) * tk].reshape(4 * tk, hidden))
-        return (sum_of_four(parts) * slope).astype(bf16)
-
-    hg_a = hidden_grad(after(parts_a, up_own), 0)
-    other_a = swap(after(dy_a, partial_a)[..., feats:])
-    dy_b = jnp.stack([line_b, *pieces_of(line_b)])
+        return (sum_of_four(parts) * slopes[k].reshape(4 * tk, hidden)).astype(bf16)
+
+    slopes = silu_slope(h_mine)
+    slopes = lax.optimization_barrier([slopes[:, :tk], slopes[:, tk:]])
+
+    other_a = swap(after(dy_a, h_other)[..., feats:])
+    hg_a = hidden_grad(after(parts_a, other_a, *slopes), 0)
+    line_b = after(line_b, h_other, *pieces_a)
+    pieces_b = [line_b, *pieces_of(line_b)]
+    dy_b = jnp.stack(pieces_b)
+    other_b = swap(dy_b[..., feats:])
     partial_b = down_product(dy_b)
-    all_a = after(exchange_z(four(hg_a)), partial_b, other_a)
+    sent_b = after(partial_b, other_b)
+    parts_b = [take(partial_b, z)]
+    for d in (1, 2, 3):
+        parts_b.append(lax.ppermute(take(sent_b, ahead(z, d)), "z", [(i, (i + d) % 4) for i in range(4)]))
+    all_a = after(exchange_z(four(hg_a)), partial_b)
+
     line_x = after(line_x, hg_a, dy_b)
-    x_lines = [line_x, *pieces_of(line_x)]
-
-    parts_b = exchange_z(after(partial_b, all_a))
-    out_a = up_product(all_a)
-    hg_b = hidden_grad(after(parts_b, out_a, *x_lines), 1)
-    other_b = swap(after(dy_b, out_a)[..., feats:])
+    x_1, x_3 = plane(-1, line_x), plane(-3, line_x)
+    x_2 = plane(-2, after(line_x, x_1, x_3))
+    down_grad = slot_grads(
+        down_slots, place_of, [h_own, h_other], pieces_a + pieces_b, [other_a, other_b], down_noise[0], True
+    )
+    hg_b = hidden_grad([after(parts_b[0], all_a, down_grad, x_1, x_3)] + parts_b[1:], 1)
+    out_a = up_product(after(all_a, hg_b))
     own_a, *sent_a = lax.optimization_barrier([out_a[d] for d in range(4)])
     sum_a = add_up([own_a] + [plane(d, sent_a[d - 1]) for d in (1, 2, 3)]).astype(bf16)
-    all_b = after(exchange_z(four(hg_b)), other_b, sum_a)
+    hgs = [hg.reshape(4, 4, tk, hidden) for hg in (all_a, exchange_z(four(hg_b)))]
+    other_hg = swap(hgs[0])
+    all_b = after(hgs[1], other_hg, x_2, *sent_a)
     out_b = up_product(all_b)
     own_b, *sent_b = lax.optimization_barrier([out_b[d] for d in range(4)])
-    mine_a = sum_of_four(exchange_first(after(sum_a, all_b)))
-    down_grad = slot_grads(
-        down_slots, place_of, [h_own, h_other], [dy_a, dy_b], [other_a, other_b], down_noise[0], True
-    )
-    hgs = [hg.reshape(4, 4, tk, hidden) for hg in (all_a, all_b)]
-    other_hgs = [swap(hg) for hg in hgs]
-    sent_b = [after(plane(d, sent_b[d - 1]), down_grad, mine_a, *other_hgs) for d in (1, 2, 3)]
-    sum_b = add_up([own_b] + sent_b).astype(bf16)
-    x_lines = [line_x.reshape(4, 2, half, feats) for line_x in x_lines]
-    up_grad = slot_grads(up_slots, place_of, x_lines, hgs, other_hgs, up_noise[0], False)
-    mine_b = sum_of_four(after(exchange_first(sum_b), up_grad))
-    mine = jnp.concatenate([mine_a, mine_b], 0).astype(bf16)
+    x_lines = [line_x.reshape(4, 2, half, feats) for line_x in (line_x, x_1, x_2, x_3)]
+    up_grad = slot_grads(up_slots, place_of, x_lines, [hgs[0], all_b], [other_hg, swap(all_b)], up_noise[0], False)
+    sum_b = add_up([own_b] + [after(plane(d, sent_b[d - 1]), up_grad) for d in (1, 2, 3)]).astype(bf16)
+    summed = exchange_first(jnp.concatenate([sum_a, sum_b], 1))
+    mine = sum_of_four(summed).astype(bf16)
     input_grad = jnp.zeros((2, half, feats), bf16)
     input_grad = put(input_grad, mine[None, :, :feats], (c, 0, 0))
     input_grad = put(input_grad, swap(mine[:, feats:])[None], (other_c, 0, 0))

time: 191 us -> 176 us (0.921)
  waiting for transfers between devices: 36.7 us -> 26.2 us
  Pallas kernels: 22.7 us -> 31.1 us
  starting transfers between devices: 69.6 us -> 61.2 us
  other arithmetic: 15.4 us -> 8.27 us
  local copies, waits for them, and re-layouts: 22.4 us -> 27.4 us
    all_to_all x5 -> x4, waiting for transfers between devices: 26.2 us -> 6.53 us  [exchange_z(): return lax.all_to_all(value, 'z', 0, 0, tiled=True)]
    all_to_all x2 -> x1, waiting for transfers between devices: 0.01 us -> 10 us  [exchange_first(): lax.all_to_all(value, PLANE, 0, 0, axis_index_groups=lines, tiled=True)]
    ppermute x18, starting transfers between devices: 25 us -> 18.4 us  [along(): return lax.ppermute(value, PLANE, pairs)]
    pallas_call x2, Pallas kernels: 15 us -> 20.8 us  [slot_grads(): pl.pallas_call(functools.partial(grads_kernel, down, len(lefts), len(owns...]
    all_to_all x2 -> x1, starting transfers between devices: 7.61 us -> 3.55 us  [exchange_first(): lax.all_to_all(value, PLANE, 0, 0, axis_index_groups=lines, tiled=True)]
    ppermute x0 -> x3, starting transfers between devices: none -> 4.01 us  [on_device(): lax.ppermute(take(sent_b, ahead(z, d)), 'z', [(i, (i + d) % 4) for i in r...]
    all_to_all x5 -> x4, starting transfers between devices: 21.3 us -> 18 us  [exchange_z(): return lax.all_to_all(value, 'z', 0, 0, tiled=True)]
    another operation x2 -> x1, other arithmetic: 2.91 us -> 0.26 us  [on_device(): dy_a = jnp.stack(pieces_a)]
  transfers between devices with their start and end apart: 34 -> 35, of which waited for: 10 -> 9; matrix products, arithmetic and copies ran while one was open for 27% -> 27% of each run, Pallas kernels for 12% -> 18%
where the time goes in v1:
time: 176 us; the launch traced here: 175 us
  starting transfers between devices  61.2 us (35%)
  Pallas kernels  31.1 us (18%)
  local copies, waits for them, and re-layouts  27.4 us (16%)
  waiting for transfers between devices  26.2 us (15%)
  matrix products  19.7 us (11%)
  other arithmetic  8.27 us (5%)
    pallas_call x2, Pallas kernels, slot_grads(): pl.pallas_call(functools.partial(grads_kernel, down, len(lefts), len(owns...  20.8 us
    dot_general x4, matrix products, dot(): lax.dot_general(a, b, (contract, ((), ())), preferred_element_type=jnp.fl...  19.7 us
    ppermute x18, starting transfers between devices, along(): return lax.ppermute(value, PLANE, pairs)  18.4 us
    all_to_all x4, starting transfers between devices, exchange_z(): return lax.all_to_all(value, 'z', 0, 0, tiled=True)  18 us
    ppermute x9, starting transfers between devices, swap(): return lax.ppermute(value, 'c', [(0, 1), (1, 0)])  17.2 us
    pallas_call x2, Pallas kernels, dense_weights(): pl.pallas_call(weights_kernel, grid_spec=pltpu.PrefetchScalarGridSpec(num...  10.3 us
    all_to_all x1, waiting for transfers between devices, exchange_first(): lax.all_to_all(value, PLANE, 0, 0, axis_index_groups=lines, tiled=True)  10 us
    ppermute x18, waiting for transfers between devices, along(): return lax.ppermute(value, PLANE, pairs)  7.11 us
  transfers between devices with their start and end apart: 35, of which 9 were waited for; matrix products, arithmetic and copies ran while one was open for 27% of the time, Pallas kernels for 18%

profile of v1, /device:TPU:1, one launch (start us, length us, event | category | flops | bytes accessed | tf_op | source)
XLA Modules:
  0.0 175.1 jit_solution(6913064553004665706)
XLA Ops:
  5.0 2.9 %collective-permute-start.1 = (bf16[256,1024]{1,0:T(8,128)(2,1)S(1)}, bf16[256,1024]{1,0:T(8,128)(2,1)S(1)}, u32[]{:S(2)}, u32[]{:S(2)}) collective-permute-start(bf16[256,1024]{1,0:T(8,128)(2,1)S(1)} %pad_maximum_fusion.13), channel_id=1, source_target_pairs={{0,12},{1,13},{2,14},{3,15},{4,0},{5,1},{6,2},{7,3},{8,4},{9,5},{1... | collective-permute-start | bytes 1572872 | tf_op jit(solution)/shard_map/ppermute | solution.py:22
  10.5 5.0 %all-to-all-start = ((bf16[4,256,1024]{2,1,0:T(8,128)(2,1)}), bf16[4,256,1024]{2,1,0:T(8,128)(2,1)}, u32[]{:S(2)}, u32[]{:S(2)}) async-start(bf16[4,256,1024]{2,1,0:T(8,128)(2,1)} %broadcast_in_dim.84), calls=%async_computation | async-start | bytes 4194304 | tf_op jit(solution)/shard_map/all_to_all | solution.py:36
  15.5 5.1 %dense_weights.2 = bf16[1024,1024]{1,0:T(8,128)(2,1)} custom-call(s32[4]{0:T(128)} %bitcast.161, bf16[4,512,512]{2,1,0:T(8,128)(2,1)} %bitcast.170, bf16[4,512,512]{2,1,0:T(8,128)(2,1)} %bitcast.165), custom_call_target="tpu_custom_call" | custom-call | flops 2097152 | bytes 6291456 | tf_op jit(solution)/shard_map/dense_weights/pallas_call | solution.py:102
  25.5 2.5 %collective-permute-start.5 = (bf16[4,32,2048]{2,1,0:T(8,128)(2,1)S(1)}, bf16[4,32,2048]{2,1,0:T(8,128)(2,1)S(1)}, u32[]{:S(2)}, u32[]{:S(2)}) collective-permute-start(bf16[4,32,2048]{2,1,0:T(8,128)(2,1)S(1)} %fusion.19.refs_2_), channel_id=1, source_target_pairs={{0,2},{1,3},{2,0},{3,1},{4,6},{5,7},{6,4},{7,5},{8,10},{9,11},{10,... | collective-permute-start | bytes 1572872 | tf_op jit(solution)/shard_map/ppermute | solution.py:22
  32.6 5.2 %dense_weights.3 = bf16[1024,1024]{1,0:T(8,128)(2,1)} custom-call(s32[4]{0:T(128)} %bitcast.163, bf16[4,512,512]{2,1,0:T(8,128)(2,1)} %bitcast.171, bf16[4,512,512]{2,1,0:T(8,128)(2,1)} %bitcast.172), custom_call_target="tpu_custom_call" | custom-call | flops 2097152 | bytes 6291456 | tf_op jit(solution)/shard_map/dense_weights/pallas_call | solution.py:102
  42.9 4.9 %fusion.2 = bf16[512,1024]{1,0:T(8,128)(2,1)} fusion(bf16[512,2048]{1,0:T(8,128)(2,1)S(1)} %bitcast.167, bf16[1024,1024]{1,0:T(8,128)(2,1)} %collective-permute-done.7, bf16[1024,1024]{1,0:T(8,128)(2,1)S(1)} %copy-done.9), kind=kOutput, calls=%fused_computation.8 | convolution fusion | flops 2156396544 | bytes 7340032 | tf_op jit(solution)/shard_map/dot_general | solution.py:221
  49.8 5.0 %all-to-all-start.1 = ((bf16[4,128,1024]{2,1,0:T(8,128)(2,1)}), bf16[4,128,1024]{2,1,0:T(8,128)(2,1)}, u32[]{:S(2)}, u32[]{:S(2)}) async-start(bf16[4,128,1024]{2,1,0:T(8,128)(2,1)} %bitcast.179), calls=%async_computation.1 | async-start | bytes 2097152 | tf_op jit(solution)/shard_map/all_to_all | solution.py:36
  60.9 3.6 %collective-permute-start.9 = (bf16[4,4,32,1024]{3,2,1,0:T(8,128)(2,1)}, bf16[4,4,32,1024]{3,2,1,0:T(8,128)(2,1)}, u32[]{:S(2)}, u32[]{:S(2)}) collective-permute-start(bf16[4,4,32,1024]{3,2,1,0:T(8,128)(2,1)} %slice.196), channel_id=1, source_target_pairs={{0,16},{16,0},{1,17},{17,1},{2,18},{18,2},{3,19},{19,3},{4,20},{20... | collective-permute-start | bytes 3145736 | tf_op jit(solution)/shard_map/ppermute | solution.py:44
  67.7 2.5 %collective-permute-done.12.refs_9_ = bf16[4,32,2048]{2,1,0:T(8,128)(2,1)S(1)} collective-permute-done((bf16[4,32,2048]{2,1,0:T(8,128)(2,1)S(1)}, bf16[4,32,2048]{2,1,0:T(8,128)(2,1)S(1)}, u32[]{:S(2)}, u32[]{:S(2)}) %collective-permute-start.12) | collective-permute-done | bytes 524320 | tf_op jit(solution)/shard_map/ppermute | solution.py:22
  72.7 1.9 %collective-permute-start.13 = (bf16[4,4,32,1024]{3,2,1,0:T(8,128)(2,1)}, bf16[4,4,32,1024]{3,2,1,0:T(8,128)(2,1)}, u32[]{:S(2)}, u32[]{:S(2)}) collective-permute-start(bf16[4,4,32,1024]{3,2,1,0:T(8,128)(2,1)} %slice.238), channel_id=1, source_target_pairs={{0,16},{16,0},{1,17},{17,1},{2,18},{18,2},{3,19},{19,3},{4,20},{20... | collective-permute-start | bytes 3145736 | tf_op jit(solution)/shard_map/ppermute | solution.py:44
  79.8 4.5 %all-to-all-start.2 = ((bf16[4,128,1024]{2,1,0:T(8,128)(2,1)}), bf16[4,128,1024]{2,1,0:T(8,128)(2,1)}, u32[]{:S(2)}, u32[]{:S(2)}) async-start(bf16[4,128,1024]{2,1,0:T(8,128)(2,1)} %broadcast_in_dim.86), calls=%async_computation.2 | async-start | bytes 2097152 | tf_op jit(solution)/shard_map/all_to_all | solution.py:36
  84.2 5.2 %fusion.3 = bf16[512,1024]{1,0:T(8,128)(2,1)S(1)} fusion(bf16[512,2048]{1,0:T(8,128)(2,1)} %bitcast.168, bf16[1024,1024]{1,0:T(8,128)(2,1)} %collective-permute-done.7, bf16[1024,1024]{1,0:T(8,128)(2,1)} %dense_weights.2), kind=kOutput, calls=%fused_computation.9 | convolution fusion | flops 2156396544 | bytes 7340032 | tf_op jit(solution)/shard_map/dot_general | solution.py:221
  90.4 2.9 %collective-permute-start.18 = (bf16[128,1024]{1,0:T(8,128)(2,1)}, bf16[128,1024]{1,0:T(8,128)(2,1)}, u32[]{:S(2)}, u32[]{:S(2)}) collective-permute-start(bf16[128,1024]{1,0:T(8,128)(2,1)} %get-tuple-element.86), channel_id=1, source_target_pairs={{0,96},{32,0},{64,32},{96,64},{1,97},{33,1},{65,33},{97,65},{2,98}... | collective-permute-start | bytes 786440 | tf_op jit(solution)/shard_map/ppermute | solution.py:306
  95.0 11.4 %slot_grads.2 = f32[4,512,512]{2,1,0:T(8,128)} custom-call(s32[4]{0:T(128)S(1)} %bitcast.162, s32[3]{0:T(128)S(1)} %add_convert_fusion.3.place_of, bf16[4,2,2,64,1024]{4,3,2,1,0:T(8,128)(2,1)} %bitcast.26.refs_0_, bf16[4,2,2,64,1024]{4,3,2,1,0:T(8,128)(2,1)} %collective-permute-done.8.refs_1_, bf16[4,32,2048]{2,1,0:T(8,128)(2,1)S(1)} %fusion.19.refs_2_, ...), custom_call_target="tpu_custom_call" | custom-call | flops 4294967296 | bytes 14680064 | tf_op jit(solution)/shard_map/slot_grads/pallas_call | solution.py:202
  106.4 3.3 %collective-permute-start.23 = (bf16[4,4,32,1024]{3,2,1,0:T(8,128)(2,1)}, bf16[4,4,32,1024]{3,2,1,0:T(8,128)(2,1)S(1)}, u32[]{:S(2)}, u32[]{:S(2)}) collective-permute-start(bf16[4,4,32,1024]{3,2,1,0:T(8,128)(2,1)} %bitcast.62.refs_4_), channel_id=1, source_target_pairs={{0,16},{16,0},{1,17},{17,1},{2,18},{18,2},{3,19},{19,3},{4,20},{20... | collective-permute-start | bytes 3145736 | tf_op jit(solution)/shard_map/ppermute | solution.py:44
  113.8 3.5 %all-to-all-start.3 = ((bf16[4,128,1024]{2,1,0:T(8,128)(2,1)}), bf16[4,128,1024]{2,1,0:T(8,128)(2,1)S(1)}, u32[]{:S(2)}, u32[]{:S(2)}) async-start(bf16[4,128,1024]{2,1,0:T(8,128)(2,1)} %broadcast_in_dim.91), calls=%async_computation.3 | async-start | bytes 2097152 | tf_op jit(solution)/shard_map/all_to_all | solution.py:36
  117.4 4.9 %convolution_convert_fusion.1 = bf16[512,2048]{1,0:T(8,128)(2,1)S(1)} fusion(bf16[512,1024]{1,0:T(8,128)(2,1)} %bitcast.56, bf16[1024,1024]{1,0:T(8,128)(2,1)} %collective-permute-done.19, bf16[1024,1024]{1,0:T(8,128)(2,1)} %dense_weights.3), kind=kOutput, calls=%fused_computation.3 | convolution fusion | flops 2156920832 | bytes 7340032 | tf_op jit(solution)/shard_map/dot_general | solution.py:221
  125.6 6.5 %all-to-all-done.3 = bf16[4,128,1024]{2,1,0:T(8,128)(2,1)S(1)} async-done(((bf16[4,128,1024]{2,1,0:T(8,128)(2,1)}), bf16[4,128,1024]{2,1,0:T(8,128)(2,1)S(1)}, u32[]{:S(2)}, u32[]{:S(2)}) %all-to-all-start.3) | async-done | bytes 1048608 | tf_op jit(solution)/shard_map/all_to_all | solution.py:36
  133.4 4.6 %convolution_convert_fusion = bf16[512,2048]{1,0:T(8,128)(2,1)S(1)} fusion(bf16[512,1024]{1,0:T(8,128)(2,1)S(1)} %bitcast.159, bf16[1024,1024]{1,0:T(8,128)(2,1)} %collective-permute-done.19, bf16[1024,1024]{1,0:T(8,128)(2,1)} %dense_weights.3), kind=kOutput, calls=%fused_computation.2 | convolution fusion | flops 2156920832 | bytes 7340032 | tf_op jit(solution)/shard_map/dot_general | solution.py:221
  143.7 9.4 %slot_grads.3 = f32[4,512,512]{2,1,0:T(8,128)} custom-call(s32[4]{0:T(128)S(1)} %bitcast.164, s32[3]{0:T(128)S(1)} %add_convert_fusion.3.place_of, bf16[4,2,64,1024]{3,2,1,0:T(8,128)(2,1)} %bitcast.68.refs_0_, bf16[4,2,64,1024]{3,2,1,0:T(8,128)(2,1)} %bitcast.69.refs_1_, bf16[4,2,64,1024]{3,2,1,0:T(8,128)(2,1)} %bitcast.70.refs_2_, ...), custom_call_target="tpu_custom_call" | custom-call | flops 4294967296 | bytes 14680064 | tf_op jit(solution)/shard_map/slot_grads/pallas_call | solution.py:202
  153.1 2.2 %collective-permute-done.25 = bf16[4,32,2048]{2,1,0:T(8,128)(2,1)S(1)} collective-permute-done((bf16[4,32,2048]{2,1,0:T(8,128)(2,1)S(1)}, bf16[4,32,2048]{2,1,0:T(8,128)(2,1)S(1)}, u32[]{:S(2)}, u32[]{:S(2)}) %collective-permute-start.25) | collective-permute-done | bytes 524320 | tf_op jit(solution)/shard_map/ppermute | solution.py:22
  156.8 3.6 %all-to-all-start.4 = ((bf16[4,64,2048]{2,1,0:T(8,128)(2,1)}), bf16[4,64,2048]{2,1,0:T(8,128)(2,1)S(1)}, u32[]{:S(2)}, u32[]{:S(2)}) async-start(bf16[4,64,2048]{2,1,0:T(8,128)(2,1)} %pad_maximum_fusion.12), calls=%async_computation.4 | async-start | bytes 2097152 | tf_op jit(solution)/shard_map/all_to_all | solution.py:32
  160.3 10.0 %all-to-all-done.4 = bf16[4,64,2048]{2,1,0:T(8,128)(2,1)S(1)} async-done(((bf16[4,64,2048]{2,1,0:T(8,128)(2,1)}), bf16[4,64,2048]{2,1,0:T(8,128)(2,1)S(1)}, u32[]{:S(2)}, u32[]{:S(2)}) %all-to-all-start.4) | async-done | bytes 1048608 | tf_op jit(solution)/shard_map/all_to_all | solution.py:32
  170.5 2.8 %collective-permute-start.29 = (bf16[64,1024]{1,0:T(8,128)(2,1)S(1)}, bf16[64,1024]{1,0:T(8,128)(2,1)S(1)}, u32[]{:S(2)}, u32[]{:S(2)}) collective-permute-start(bf16[64,1024]{1,0:T(8,128)(2,1)S(1)} %slice.252), channel_id=1, source_target_pairs={{0,16},{16,0},{1,17},{17,1},{2,18},{18,2},{3,19},{19,3},{4,20},{20... | collective-permute-start | bytes 393224 | tf_op jit(solution)/shard_map/ppermute | solution.py:44
  (140 shorter events, 60.5 us)
Async XLA Ops:
  5.0 16.8 %collective-permute-start.1 = (bf16[256,1024]{1,0:T(8,128)(2,1)S(1)}, bf16[256,1024]{1,0:T(8,128)(2,1)S(1)}, u32[]{:S(2)}, u32[]{:S(2)}) collective-permute-start(bf16[256,1024]{1,0:T(8,128)(2,1)S(1)} %pad_maximum_fusion.13), channel_id=1, source_target_pairs={{0,12},{1,13},{2,14},{3,15},{4,0},{5,1},{6,2},{7,3},{8,4},{9,5},{1... | collective-permute-start | bytes 1572872 | tf_op jit(solution)/shard_map/ppermute | solution.py:22
  8.2 15.2 %collective-permute-start.3 = (bf16[256,1024]{1,0:T(8,128)(2,1)S(1)}, bf16[256,1024]{1,0:T(8,128)(2,1)S(1)}, u32[]{:S(2)}, u32[]{:S(2)}) collective-permute-start(bf16[256,1024]{1,0:T(8,128)(2,1)S(1)} %pad_maximum_fusion.13), channel_id=1, source_target_pairs={{0,4},{1,5},{2,6},{3,7},{4,8},{5,9},{6,10},{7,11},{8,12},{9,13},{1... | collective-permute-start | bytes 1572872 | tf_op jit(solution)/shard_map/ppermute | solution.py:22
  10.5 37.3 %all-to-all-start = ((bf16[4,256,1024]{2,1,0:T(8,128)(2,1)}), bf16[4,256,1024]{2,1,0:T(8,128)(2,1)}, u32[]{:S(2)}, u32[]{:S(2)}) async-start(bf16[4,256,1024]{2,1,0:T(8,128)(2,1)} %broadcast_in_dim.84), calls=%async_computation | async-start | bytes 4194304 | tf_op jit(solution)/shard_map/all_to_all | solution.py:36
  20.6 20.2 %collective-permute-start.7 = (bf16[1024,1024]{1,0:T(8,128)(2,1)}, bf16[1024,1024]{1,0:T(8,128)(2,1)}, u32[]{:S(2)}, u32[]{:S(2)}) collective-permute-start(bf16[1024,1024]{1,0:T(8,128)(2,1)} %dense_weights.2), channel_id=1, source_target_pairs={{0,16},{16,0},{1,17},{17,1},{2,18},{18,2},{3,19},{19,3},{4,20},{20... | collective-permute-start | bytes 6291464 | tf_op jit(solution)/shard_map/ppermute | solution.py:44
  24.3 15.9 %collective-permute-start.6 = (bf16[4,32,2048]{2,1,0:T(8,128)(2,1)S(1)}, bf16[4,32,2048]{2,1,0:T(8,128)(2,1)S(1)}, u32[]{:S(2)}, u32[]{:S(2)}) collective-permute-start(bf16[4,32,2048]{2,1,0:T(8,128)(2,1)S(1)} %fusion.19.refs_2_), channel_id=1, source_target_pairs={{0,1},{1,2},{2,3},{3,0},{4,5},{5,6},{6,7},{7,4},{8,9},{9,10},{10,1... | collective-permute-start | bytes 1572872 | tf_op jit(solution)/shard_map/ppermute | solution.py:22
  49.7 67.6 %collective-permute-start.19 = (bf16[1024,1024]{1,0:T(8,128)(2,1)}, bf16[1024,1024]{1,0:T(8,128)(2,1)}, u32[]{:S(2)}, u32[]{:S(2)}) collective-permute-start(bf16[1024,1024]{1,0:T(8,128)(2,1)} %dense_weights.3), channel_id=1, source_target_pairs={{0,16},{16,0},{1,17},{17,1},{2,18},{18,2},{3,19},{19,3},{4,20},{20... | collective-permute-start | bytes 6291464 | tf_op jit(solution)/shard_map/ppermute | solution.py:44
  49.8 27.3 %all-to-all-start.1 = ((bf16[4,128,1024]{2,1,0:T(8,128)(2,1)}), bf16[4,128,1024]{2,1,0:T(8,128)(2,1)}, u32[]{:S(2)}, u32[]{:S(2)}) async-start(bf16[4,128,1024]{2,1,0:T(8,128)(2,1)} %bitcast.179), calls=%async_computation.1 | async-start | bytes 2097152 | tf_op jit(solution)/shard_map/all_to_all | solution.py:36
  54.8 15.3 %collective-permute-start.12 = (bf16[4,32,2048]{2,1,0:T(8,128)(2,1)S(1)}, bf16[4,32,2048]{2,1,0:T(8,128)(2,1)S(1)}, u32[]{:S(2)}, u32[]{:S(2)}) collective-permute-start(bf16[4,32,2048]{2,1,0:T(8,128)(2,1)S(1)} %fusion.23.refs_6_), channel_id=1, source_target_pairs={{0,1},{1,2},{2,3},{3,0},{4,5},{5,6},{6,7},{7,4},{8,9},{9,10},{10,1... | collective-permute-start | bytes 1572872 | tf_op jit(solution)/shard_map/ppermute | solution.py:22
  54.9 15.2 %collective-permute-start.11 = (bf16[4,32,2048]{2,1,0:T(8,128)(2,1)S(1)}, bf16[4,32,2048]{2,1,0:T(8,128)(2,1)S(1)}, u32[]{:S(2)}, u32[]{:S(2)}) collective-permute-start(bf16[4,32,2048]{2,1,0:T(8,128)(2,1)S(1)} %fusion.23.refs_6_), channel_id=1, source_target_pairs={{0,2},{1,3},{2,0},{3,1},{4,6},{5,7},{6,4},{7,5},{8,10},{9,11},{10,... | collective-permute-start | bytes 1572872 | tf_op jit(solution)/shard_map/ppermute | solution.py:22
  60.9 16.2 %collective-permute-start.9 = (bf16[4,4,32,1024]{3,2,1,0:T(8,128)(2,1)}, bf16[4,4,32,1024]{3,2,1,0:T(8,128)(2,1)}, u32[]{:S(2)}, u32[]{:S(2)}) collective-permute-start(bf16[4,4,32,1024]{3,2,1,0:T(8,128)(2,1)} %slice.196), channel_id=1, source_target_pairs={{0,16},{16,0},{1,17},{17,1},{2,18},{18,2},{3,19},{19,3},{4,20},{20... | collective-permute-start | bytes 3145736 | tf_op jit(solution)/shard_map/ppermute | solution.py:44
  72.7 16.8 %collective-permute-start.13 = (bf16[4,4,32,1024]{3,2,1,0:T(8,128)(2,1)}, bf16[4,4,32,1024]{3,2,1,0:T(8,128)(2,1)}, u32[]{:S(2)}, u32[]{:S(2)}) collective-permute-start(bf16[4,4,32,1024]{3,2,1,0:T(8,128)(2,1)} %slice.238), channel_id=1, source_target_pairs={{0,16},{16,0},{1,17},{17,1},{2,18},{18,2},{3,19},{19,3},{4,20},{20... | collective-permute-start | bytes 3145736 | tf_op jit(solution)/shard_map/ppermute | solution.py:44
  75.6 18.3 %collective-permute-start.14 = (bf16[4,128,1024]{2,1,0:T(8,128)(2,1)}, bf16[4,128,1024]{2,1,0:T(8,128)(2,1)}, u32[]{:S(2)}, u32[]{:S(2)}) collective-permute-start(bf16[4,128,1024]{2,1,0:T(8,128)(2,1)} %bitcast_dynamic-update-slice_fusion), channel_id=1, source_target_pairs={{0,3},{1,0},{2,1},{3,2},{4,7},{5,4},{6,5},{7,6},{8,11},{9,8},{10,9... | collective-permute-start | bytes 3145736 | tf_op jit(solution)/shard_map/ppermute | solution.py:22
  76.0 18.5 %collective-permute-start.15 = (bf16[4,128,1024]{2,1,0:T(8,128)(2,1)}, bf16[4,128,1024]{2,1,0:T(8,128)(2,1)}, u32[]{:S(2)}, u32[]{:S(2)}) collective-permute-start(bf16[4,128,1024]{2,1,0:T(8,128)(2,1)} %bitcast_dynamic-update-slice_fusion), channel_id=1, source_target_pairs={{0,1},{1,2},{2,3},{3,0},{4,5},{5,6},{6,7},{7,4},{8,9},{9,10},{10,1... | collective-permute-start | bytes 3145736 | tf_op jit(solution)/shard_map/ppermute | solution.py:22
  79.8 26.7 %all-to-all-start.2 = ((bf16[4,128,1024]{2,1,0:T(8,128)(2,1)}), bf16[4,128,1024]{2,1,0:T(8,128)(2,1)}, u32[]{:S(2)}, u32[]{:S(2)}) async-start(bf16[4,128,1024]{2,1,0:T(8,128)(2,1)} %broadcast_in_dim.86), calls=%async_computation.2 | async-start | bytes 2097152 | tf_op jit(solution)/shard_map/all_to_all | solution.py:36
  90.4 16.0 %collective-permute-start.18 = (bf16[128,1024]{1,0:T(8,128)(2,1)}, bf16[128,1024]{1,0:T(8,128)(2,1)}, u32[]{:S(2)}, u32[]{:S(2)}) collective-permute-start(bf16[128,1024]{1,0:T(8,128)(2,1)} %get-tuple-element.86), channel_id=1, source_target_pairs={{0,96},{32,0},{64,32},{96,64},{1,97},{33,1},{65,33},{97,65},{2,98}... | collective-permute-start | bytes 786440 | tf_op jit(solution)/shard_map/ppermute | solution.py:306
  93.3 16.4 %collective-permute-start.17 = (bf16[128,1024]{1,0:T(8,128)(2,1)}, bf16[128,1024]{1,0:T(8,128)(2,1)}, u32[]{:S(2)}, u32[]{:S(2)}) collective-permute-start(bf16[128,1024]{1,0:T(8,128)(2,1)} %get-tuple-element.87), channel_id=1, source_target_pairs={{0,64},{32,96},{64,0},{96,32},{1,65},{33,97},{65,1},{97,33},{2,66}... | collective-permute-start | bytes 786440 | tf_op jit(solution)/shard_map/ppermute | solution.py:306
  93.9 17.4 %collective-permute-start.16 = (bf16[128,1024]{1,0:T(8,128)(2,1)}, bf16[128,1024]{1,0:T(8,128)(2,1)}, u32[]{:S(2)}, u32[]{:S(2)}) collective-permute-start(bf16[128,1024]{1,0:T(8,128)(2,1)} %get-tuple-element.85), channel_id=1, source_target_pairs={{0,32},{32,64},{64,96},{96,0},{1,33},{33,65},{65,97},{97,1},{2,34}... | collective-permute-start | bytes 786440 | tf_op jit(solution)/shard_map/ppermute | solution.py:306
  94.5 31.1 %collective-permute-start.24 = (bf16[4,128,1024]{2,1,0:T(8,128)(2,1)}, bf16[4,128,1024]{2,1,0:T(8,128)(2,1)}, u32[]{:S(2)}, u32[]{:S(2)}) collective-permute-start(bf16[4,128,1024]{2,1,0:T(8,128)(2,1)} %bitcast_dynamic-update-slice_fusion), channel_id=1, source_target_pairs={{0,2},{1,3},{2,0},{3,1},{4,6},{5,7},{6,4},{7,5},{8,10},{9,11},{10,... | collective-permute-start | bytes 3145736 | tf_op jit(solution)/shard_map/ppermute | solution.py:22
  106.4 25.7 %collective-permute-start.23 = (bf16[4,4,32,1024]{3,2,1,0:T(8,128)(2,1)}, bf16[4,4,32,1024]{3,2,1,0:T(8,128)(2,1)S(1)}, u32[]{:S(2)}, u32[]{:S(2)}) collective-permute-start(bf16[4,4,32,1024]{3,2,1,0:T(8,128)(2,1)} %bitcast.62.refs_4_), channel_id=1, source_target_pairs={{0,16},{16,0},{1,17},{17,1},{2,18},{18,2},{3,19},{19,3},{4,20},{20... | collective-permute-start | bytes 3145736 | tf_op jit(solution)/shard_map/ppermute | solution.py:44
  113.8 18.3 %all-to-all-start.3 = ((bf16[4,128,1024]{2,1,0:T(8,128)(2,1)}), bf16[4,128,1024]{2,1,0:T(8,128)(2,1)S(1)}, u32[]{:S(2)}, u32[]{:S(2)}) async-start(bf16[4,128,1024]{2,1,0:T(8,128)(2,1)} %broadcast_in_dim.91), calls=%async_computation.3 | async-start | bytes 2097152 | tf_op jit(solution)/shard_map/all_to_all | solution.py:36
  123.5 16.4 %collective-permute-start.22 = (bf16[4,32,2048]{2,1,0:T(8,128)(2,1)}, bf16[4,32,2048]{2,1,0:T(8,128)(2,1)S(1)}, u32[]{:S(2)}, u32[]{:S(2)}) collective-permute-start(bf16[4,32,2048]{2,1,0:T(8,128)(2,1)} %bitcast.60), channel_id=1, source_target_pairs={{0,3},{1,0},{2,1},{3,2},{4,7},{5,4},{6,5},{7,6},{8,11},{9,8},{10,9... | collective-permute-start | bytes 1572872 | tf_op jit(solution)/shard_map/ppermute | solution.py:22
  125.0 15.1 %collective-permute-start.21 = (bf16[4,32,2048]{2,1,0:T(8,128)(2,1)}, bf16[4,32,2048]{2,1,0:T(8,128)(2,1)}, u32[]{:S(2)}, u32[]{:S(2)}) collective-permute-start(bf16[4,32,2048]{2,1,0:T(8,128)(2,1)} %bitcast.59), channel_id=1, source_target_pairs={{0,2},{1,3},{2,0},{3,1},{4,6},{5,7},{6,4},{7,5},{8,10},{9,11},{10,... | collective-permute-start | bytes 1572872 | tf_op jit(solution)/shard_map/ppermute | solution.py:22
  125.3 15.8 %collective-permute-start.20 = (bf16[4,32,2048]{2,1,0:T(8,128)(2,1)}, bf16[4,32,2048]{2,1,0:T(8,128)(2,1)}, u32[]{:S(2)}, u32[]{:S(2)}) collective-permute-start(bf16[4,32,2048]{2,1,0:T(8,128)(2,1)} %bitcast.58), channel_id=1, source_target_pairs={{0,1},{1,2},{2,3},{3,0},{4,5},{5,6},{6,7},{7,4},{8,9},{9,10},{10,1... | collective-permute-start | bytes 1572872 | tf_op jit(solution)/shard_map/ppermute | solution.py:22
  140.1 15.2 %collective-permute-start.25 = (bf16[4,32,2048]{2,1,0:T(8,128)(2,1)S(1)}, bf16[4,32,2048]{2,1,0:T(8,128)(2,1)S(1)}, u32[]{:S(2)}, u32[]{:S(2)}) collective-permute-start(bf16[4,32,2048]{2,1,0:T(8,128)(2,1)S(1)} %bitcast.180), channel_id=1, source_target_pairs={{0,1},{1,2},{2,3},{3,0},{4,5},{5,6},{6,7},{7,4},{8,9},{9,10},{10,1... | collective-permute-start | bytes 1572872 | tf_op jit(solution)/shard_map/ppermute | solution.py:22
  (28 other events, 178.1 us)

commit v2 on v1

--- a/solution.py
+++ b/solution.py
@@ -62,6 +62,19 @@
 
 def after(value, *others):
     return lax.optimization_barrier((value, *others))[0]
+
+
+def in_turn(value, *others):
+    anywhere = pl.BlockSpec(memory_space=pl.ANY)
+    return pl.pallas_call(
+        lambda *refs: None,
+        in_specs=[anywhere] * (1 + len(others)),
+        out_specs=anywhere,
+        out_shape=jax.ShapeDtypeStruct(value.shape, value.dtype),
+        input_output_aliases={0: 0},
+        cost_estimate=pl.CostEstimate(flops=0, bytes_accessed=0, transcendentals=0),
+        name="in_turn",
+    )(value, *others)
 
 
 def silu_slope(values):
@@ -304,15 +317,16 @@
     parts_b = [take(partial_b, z)]
     for d in (1, 2, 3):
         parts_b.append(lax.ppermute(take(sent_b, ahead(z, d)), "z", [(i, (i + d) % 4) for i in range(4)]))
-    all_a = after(exchange_z(four(hg_a)), partial_b)
-
-    line_x = after(line_x, hg_a, dy_b)
+    sent_hg = four(hg_a)
+    all_a = after(exchange_z(sent_hg), partial_b)
+
+    line_x = in_turn(line_x, sent_hg)
     x_1, x_3 = plane(-1, line_x), plane(-3, line_x)
     x_2 = plane(-2, after(line_x, x_1, x_3))
     down_grad = slot_grads(
         down_slots, place_of, [h_own, h_other], pieces_a + pieces_b, [other_a, other_b], down_noise[0], True
     )
-    hg_b = hidden_grad([after(parts_b[0], all_a, down_grad, x_1, x_3)] + parts_b[1:], 1)
+    hg_b = hidden_grad([after(parts_b[0], all_a, down_grad)] + parts_b[1:], 1)
     out_a = up_product(after(all_a, hg_b))
     own_a, *sent_a = lax.optimization_barrier([out_a[d] for d in range(4)])
     sum_a = add_up([own_a] + [plane(d, sent_a[d - 1]) for d in (1, 2, 3)]).astype(bf16)

time: 176 us -> 174 us (0.989)
  local copies, waits for them, and re-layouts: 27.4 us -> 23.8 us
  Pallas kernels: 31.1 us -> 28.4 us
    ppermute x18, waiting for transfers between devices: 7.11 us -> 10.2 us  [along(): return lax.ppermute(value, PLANE, pairs)]
    all_to_all x4, waiting for transfers between devices: 6.53 us -> 4.19 us  [exchange_z(): return lax.all_to_all(value, 'z', 0, 0, tiled=True)]
    dynamic_update_slice x6, local copies, waits for them, and re-layouts: 4.8 us -> 2.96 us  [put(): return lax.dynamic_update_slice(buffer, value, unsigned(starts))]
    unnamed x34 -> x46, local copies, waits for them, and re-layouts: 5.12 us -> 4.05 us
  transfers between devices with their start and end apart: 35 -> 35, of which waited for: 9 -> 9; matrix products, arithmetic and copies ran while one was open for 27% -> 27% of each run, Pallas kernels for 18% -> 16%
where the time goes in v2:
time: 174 us; the launch traced here: 173 us
  starting transfers between devices  62.5 us (36%)
  Pallas kernels  28.4 us (16%)
  waiting for transfers between devices  27.7 us (16%)
  local copies, waits for them, and re-layouts  23.8 us (14%)
  matrix products  19.7 us (11%)
  other arithmetic  9.31 us (5%)
    dot_general x4, matrix products, dot(): lax.dot_general(a, b, (contract, ((), ())), preferred_element_type=jnp.fl...  19.7 us
    pallas_call x2, Pallas kernels, slot_grads(): pl.pallas_call(functools.partial(grads_kernel, down, len(lefts), len(owns...  19.6 us
    ppermute x18, starting transfers between devices, along(): return lax.ppermute(value, PLANE, pairs)  19.4 us
    all_to_all x4, starting transfers between devices, exchange_z(): return lax.all_to_all(value, 'z', 0, 0, tiled=True)  18 us
    ppermute x9, starting transfers between devices, swap(): return lax.ppermute(value, 'c', [(0, 1), (1, 0)])  17.4 us
    ppermute x18, waiting for transfers between devices, along(): return lax.ppermute(value, PLANE, pairs)  10.2 us
    all_to_all x1, waiting for transfers between devices, exchange_first(): lax.all_to_all(value, PLANE, 0, 0, axis_index_groups=lines, tiled=True)  9.74 us
    pallas_call x2, Pallas kernels, dense_weights(): pl.pallas_call(weights_kernel, grid_spec=pltpu.PrefetchScalarGridSpec(num...  8.88 us
  transfers between devices with their start and end apart: 35, of which 9 were waited for; matrix products, arithmetic and copies ran while one was open for 27% of the time, Pallas kernels for 16%

profile of v2, /device:TPU:1, one launch (start us, length us, event | category | flops | bytes accessed | tf_op | source)
XLA Modules:
  0.0 172.7 jit_solution(14868976323616555459)
XLA Ops:
  5.0 2.9 %collective-permute-start.1 = (bf16[256,1024]{1,0:T(8,128)(2,1)S(1)}, bf16[256,1024]{1,0:T(8,128)(2,1)S(1)}, u32[]{:S(2)}, u32[]{:S(2)}) collective-permute-start(bf16[256,1024]{1,0:T(8,128)(2,1)S(1)} %pad_maximum_fusion.13), channel_id=1, source_target_pairs={{0,12},{1,13},{2,14},{3,15},{4,0},{5,1},{6,2},{7,3},{8,4},{9,5},{1... | collective-permute-start | bytes 1572872 | tf_op jit(solution)/shard_map/ppermute | solution.py:22
  10.5 5.0 %all-to-all-start = ((bf16[4,256,1024]{2,1,0:T(8,128)(2,1)}), bf16[4,256,1024]{2,1,0:T(8,128)(2,1)}, u32[]{:S(2)}, u32[]{:S(2)}) async-start(bf16[4,256,1024]{2,1,0:T(8,128)(2,1)} %broadcast_in_dim.84), calls=%async_computation | async-start | bytes 4194304 | tf_op jit(solution)/shard_map/all_to_all | solution.py:36
  15.5 5.0 %dense_weights.2 = bf16[1024,1024]{1,0:T(8,128)(2,1)} custom-call(s32[4]{0:T(128)} %bitcast.161, bf16[4,512,512]{2,1,0:T(8,128)(2,1)} %bitcast.170, bf16[4,512,512]{2,1,0:T(8,128)(2,1)} %bitcast.165), custom_call_target="tpu_custom_call" | custom-call | flops 2097152 | bytes 6291456 | tf_op jit(solution)/shard_map/dense_weights/pallas_call | solution.py:115
  24.8 2.5 %collective-permute-start.5 = (bf16[4,32,2048]{2,1,0:T(8,128)(2,1)S(1)}, bf16[4,32,2048]{2,1,0:T(8,128)(2,1)S(1)}, u32[]{:S(2)}, u32[]{:S(2)}) collective-permute-start(bf16[4,32,2048]{2,1,0:T(8,128)(2,1)S(1)} %fusion.19.refs_2_), channel_id=1, source_target_pairs={{0,2},{1,3},{2,0},{3,1},{4,6},{5,7},{6,4},{7,5},{8,10},{9,11},{10,... | collective-permute-start | bytes 1572872 | tf_op jit(solution)/shard_map/ppermute | solution.py:22
  29.6 3.9 %dense_weights.3 = bf16[1024,1024]{1,0:T(8,128)(2,1)} custom-call(s32[4]{0:T(128)} %bitcast.163, bf16[4,512,512]{2,1,0:T(8,128)(2,1)} %bitcast.171, bf16[4,512,512]{2,1,0:T(8,128)(2,1)} %bitcast.172), custom_call_target="tpu_custom_call" | custom-call | flops 2097152 | bytes 6291456 | tf_op jit(solution)/shard_map/dense_weights/pallas_call | solution.py:115
  35.5 4.4 %collective-permute-done.5.refs_4_ = bf16[4,32,2048]{2,1,0:T(8,128)(2,1)S(1)} collective-permute-done((bf16[4,32,2048]{2,1,0:T(8,128)(2,1)S(1)}, bf16[4,32,2048]{2,1,0:T(8,128)(2,1)S(1)}, u32[]{:S(2)}, u32[]{:S(2)}) %collective-permute-start.5) | collective-permute-done | bytes 524320 | tf_op jit(solution)/shard_map/ppermute | solution.py:22
  42.7 5.0 %fusion.2 = bf16[512,1024]{1,0:T(8,128)(2,1)} fusion(bf16[512,2048]{1,0:T(8,128)(2,1)S(1)} %bitcast.167, bf16[1024,1024]{1,0:T(8,128)(2,1)} %collective-permute-done.7, bf16[1024,1024]{1,0:T(8,128)(2,1)S(1)} %copy-done.13), kind=kOutput, calls=%fused_computation.8 | convolution fusion | flops 2156396544 | bytes 7340032 | tf_op jit(solution)/shard_map/dot_general | solution.py:234
  49.5 5.0 %all-to-all-start.1 = ((bf16[4,128,1024]{2,1,0:T(8,128)(2,1)}), bf16[4,128,1024]{2,1,0:T(8,128)(2,1)S(1)}, u32[]{:S(2)}, u32[]{:S(2)}) async-start(bf16[4,128,1024]{2,1,0:T(8,128)(2,1)} %bitcast.179), calls=%async_computation.1 | async-start | bytes 2097152 | tf_op jit(solution)/shard_map/all_to_all | solution.py:36
  61.0 3.3 %collective-permute-start.9 = (bf16[4,4,32,1024]{3,2,1,0:T(8,128)(2,1)}, bf16[4,4,32,1024]{3,2,1,0:T(8,128)(2,1)}, u32[]{:S(2)}, u32[]{:S(2)}) collective-permute-start(bf16[4,4,32,1024]{3,2,1,0:T(8,128)(2,1)} %slice.196), channel_id=1, source_target_pairs={{0,16},{16,0},{1,17},{17,1},{2,18},{18,2},{3,19},{19,3},{4,20},{20... | collective-permute-start | bytes 3145736 | tf_op jit(solution)/shard_map/ppermute | solution.py:44
  77.5 4.5 %all-to-all-start.2 = ((bf16[4,128,1024]{2,1,0:T(8,128)(2,1)}), bf16[4,128,1024]{2,1,0:T(8,128)(2,1)}, u32[]{:S(2)}, u32[]{:S(2)}) async-start(bf16[4,128,1024]{2,1,0:T(8,128)(2,1)} %broadcast_in_dim.86.refs_1_), calls=%async_computation.2 | async-start | bytes 2097152 | tf_op jit(solution)/shard_map/all_to_all | solution.py:36
  83.2 5.2 %fusion.3 = bf16[512,1024]{1,0:T(8,128)(2,1)S(1)} fusion(bf16[512,2048]{1,0:T(8,128)(2,1)} %bitcast.168, bf16[1024,1024]{1,0:T(8,128)(2,1)} %collective-permute-done.7, bf16[1024,1024]{1,0:T(8,128)(2,1)} %dense_weights.2), kind=kOutput, calls=%fused_computation.9 | convolution fusion | flops 2156396544 | bytes 7340032 | tf_op jit(solution)/shard_map/dot_general | solution.py:234
  89.4 2.9 %collective-permute-start.16 = (bf16[128,1024]{1,0:T(8,128)(2,1)}, bf16[128,1024]{1,0:T(8,128)(2,1)}, u32[]{:S(2)}, u32[]{:S(2)}) collective-permute-start(bf16[128,1024]{1,0:T(8,128)(2,1)} %get-tuple-element.84), channel_id=1, source_target_pairs={{0,96},{32,0},{64,32},{96,64},{1,97},{33,1},{65,33},{97,65},{2,98}... | collective-permute-start | bytes 786440 | tf_op jit(solution)/shard_map/ppermute | solution.py:319
  93.5 11.4 %slot_grads.2 = f32[4,512,512]{2,1,0:T(8,128)} custom-call(s32[4]{0:T(128)S(1)} %bitcast.162, s32[3]{0:T(128)S(1)} %add_convert_fusion.3.place_of, bf16[4,2,2,64,1024]{4,3,2,1,0:T(8,128)(2,1)} %bitcast.26.refs_0_, bf16[4,2,2,64,1024]{4,3,2,1,0:T(8,128)(2,1)} %collective-permute-done.8.refs_1_, bf16[4,32,2048]{2,1,0:T(8,128)(2,1)S(1)} %fusion.19.refs_2_, ...), custom_call_target="tpu_custom_call" | custom-call | flops 4294967296 | bytes 14680064 | tf_op jit(solution)/shard_map/slot_grads/pallas_call | solution.py:215
  106.4 2.5 %collective-permute-done.14 = bf16[128,1024]{1,0:T(8,128)(2,1)} collective-permute-done((bf16[128,1024]{1,0:T(8,128)(2,1)}, bf16[128,1024]{1,0:T(8,128)(2,1)}, u32[]{:S(2)}, u32[]{:S(2)}) %collective-permute-start.14) | collective-permute-done | bytes 262176 | tf_op jit(solution)/shard_map/ppermute | solution.py:319
  111.5 3.5 %all-to-all-start.3 = ((bf16[4,128,1024]{2,1,0:T(8,128)(2,1)}), bf16[4,128,1024]{2,1,0:T(8,128)(2,1)S(1)}, u32[]{:S(2)}, u32[]{:S(2)}) async-start(bf16[4,128,1024]{2,1,0:T(8,128)(2,1)} %broadcast_in_dim.91), calls=%async_computation.3 | async-start | bytes 2097152 | tf_op jit(solution)/shard_map/all_to_all | solution.py:36
  115.0 4.9 %convolution_convert_fusion.1 = bf16[512,2048]{1,0:T(8,128)(2,1)S(1)} fusion(bf16[512,1024]{1,0:T(8,128)(2,1)} %bitcast.56, bf16[1024,1024]{1,0:T(8,128)(2,1)} %collective-permute-done.17, bf16[1024,1024]{1,0:T(8,128)(2,1)} %dense_weights.3), kind=kOutput, calls=%fused_computation.3 | convolution fusion | flops 2156920832 | bytes 7340032 | tf_op jit(solution)/shard_map/dot_general | solution.py:234
  124.3 4.2 %all-to-all-done.3 = bf16[4,128,1024]{2,1,0:T(8,128)(2,1)S(1)} async-done(((bf16[4,128,1024]{2,1,0:T(8,128)(2,1)}), bf16[4,128,1024]{2,1,0:T(8,128)(2,1)S(1)}, u32[]{:S(2)}, u32[]{:S(2)}) %all-to-all-start.3) | async-done | bytes 1048608 | tf_op jit(solution)/shard_map/all_to_all | solution.py:36
  128.5 2.6 %collective-permute-start.26 = (bf16[4,4,32,1024]{3,2,1,0:T(8,128)(2,1)S(1)}, bf16[4,4,32,1024]{3,2,1,0:T(8,128)(2,1)S(1)}, u32[]{:S(2)}, u32[]{:S(2)}) collective-permute-start(bf16[4,4,32,1024]{3,2,1,0:T(8,128)(2,1)S(1)} %bitcast.158), channel_id=1, source_target_pairs={{0,16},{16,0},{1,17},{17,1},{2,18},{18,2},{3,19},{19,3},{4,20},{20... | collective-permute-start | bytes 3145736 | tf_op jit(solution)/shard_map/ppermute | solution.py:44
  131.0 4.6 %convolution_convert_fusion = bf16[512,2048]{1,0:T(8,128)(2,1)S(1)} fusion(bf16[512,1024]{1,0:T(8,128)(2,1)S(1)} %bitcast.159, bf16[1024,1024]{1,0:T(8,128)(2,1)} %collective-permute-done.17, bf16[1024,1024]{1,0:T(8,128)(2,1)} %dense_weights.3), kind=kOutput, calls=%fused_computation.2 | convolution fusion | flops 2156920832 | bytes 7340032 | tf_op jit(solution)/shard_map/dot_general | solution.py:234
  136.6 2.3 %collective-permute-start.27 = (bf16[4,32,2048]{2,1,0:T(8,128)(2,1)S(1)}, bf16[4,32,2048]{2,1,0:T(8,128)(2,1)S(1)}, u32[]{:S(2)}, u32[]{:S(2)}) collective-permute-start(bf16[4,32,2048]{2,1,0:T(8,128)(2,1)S(1)} %bitcast.181), channel_id=1, source_target_pairs={{0,2},{1,3},{2,0},{3,1},{4,6},{5,7},{6,4},{7,5},{8,10},{9,11},{10,... | collective-permute-start | bytes 1572872 | tf_op jit(solution)/shard_map/ppermute | solution.py:22
  141.6 8.2 %slot_grads.3 = f32[4,512,512]{2,1,0:T(8,128)} custom-call(s32[4]{0:T(128)S(1)} %bitcast.164, s32[3]{0:T(128)S(1)} %add_convert_fusion.3.place_of, bf16[4,2,64,1024]{3,2,1,0:T(8,128)(2,1)S(1)} %bitcast.152, bf16[4,2,64,1024]{3,2,1,0:T(8,128)(2,1)} %bitcast.69.refs_1_, bf16[4,2,64,1024]{3,2,1,0:T(8,128)(2,1)} %bitcast.70.refs_2_, ...), custom_call_target="tpu_custom_call" | custom-call | flops 4294967296 | bytes 14680064 | tf_op jit(solution)/shard_map/slot_grads/pallas_call | solution.py:215
  153.5 3.7 %all-to-all-start.4 = ((bf16[4,64,2048]{2,1,0:T(8,128)(2,1)}), bf16[4,64,2048]{2,1,0:T(8,128)(2,1)S(1)}, u32[]{:S(2)}, u32[]{:S(2)}) async-start(bf16[4,64,2048]{2,1,0:T(8,128)(2,1)} %pad_maximum_fusion.12), calls=%async_computation.4 | async-start | bytes 2097152 | tf_op jit(solution)/shard_map/all_to_all | solution.py:32
  157.1 9.7 %all-to-all-done.4 = bf16[4,64,2048]{2,1,0:T(8,128)(2,1)S(1)} async-done(((bf16[4,64,2048]{2,1,0:T(8,128)(2,1)}), bf16[4,64,2048]{2,1,0:T(8,128)(2,1)S(1)}, u32[]{:S(2)}, u32[]{:S(2)}) %all-to-all-start.4) | async-done | bytes 1048608 | tf_op jit(solution)/shard_map/all_to_all | solution.py:32
  167.0 3.9 %collective-permute-start.29 = (bf16[64,1024]{1,0:T(8,128)(2,1)S(1)}, bf16[64,1024]{1,0:T(8,128)(2,1)S(1)}, u32[]{:S(2)}, u32[]{:S(2)}) collective-permute-start(bf16[64,1024]{1,0:T(8,128)(2,1)S(1)} %slice.252), channel_id=1, source_target_pairs={{0,16},{16,0},{1,17},{17,1},{2,18},{18,2},{3,19},{19,3},{4,20},{20... | collective-permute-start | bytes 393224 | tf_op jit(solution)/shard_map/ppermute | solution.py:44
  (153 shorter events, 60.5 us)
Async XLA Ops:
  5.0 16.6 %collective-permute-start.1 = (bf16[256,1024]{1,0:T(8,128)(2,1)S(1)}, bf16[256,1024]{1,0:T(8,128)(2,1)S(1)}, u32[]{:S(2)}, u32[]{:S(2)}) collective-permute-start(bf16[256,1024]{1,0:T(8,128)(2,1)S(1)} %pad_maximum_fusion.13), channel_id=1, source_target_pairs={{0,12},{1,13},{2,14},{3,15},{4,0},{5,1},{6,2},{7,3},{8,4},{9,5},{1... | collective-permute-start | bytes 1572872 | tf_op jit(solution)/shard_map/ppermute | solution.py:22
  8.2 15.2 %collective-permute-start.3 = (bf16[256,1024]{1,0:T(8,128)(2,1)S(1)}, bf16[256,1024]{1,0:T(8,128)(2,1)S(1)}, u32[]{:S(2)}, u32[]{:S(2)}) collective-permute-start(bf16[256,1024]{1,0:T(8,128)(2,1)S(1)} %pad_maximum_fusion.13), channel_id=1, source_target_pairs={{0,4},{1,5},{2,6},{3,7},{4,8},{5,9},{6,10},{7,11},{8,12},{9,13},{1... | collective-permute-start | bytes 1572872 | tf_op jit(solution)/shard_map/ppermute | solution.py:22
  10.5 37.1 %all-to-all-start = ((bf16[4,256,1024]{2,1,0:T(8,128)(2,1)}), bf16[4,256,1024]{2,1,0:T(8,128)(2,1)}, u32[]{:S(2)}, u32[]{:S(2)}) async-start(bf16[4,256,1024]{2,1,0:T(8,128)(2,1)} %broadcast_in_dim.84), calls=%async_computation | async-start | bytes 4194304 | tf_op jit(solution)/shard_map/all_to_all | solution.py:36
  20.5 20.8 %collective-permute-start.7 = (bf16[1024,1024]{1,0:T(8,128)(2,1)}, bf16[1024,1024]{1,0:T(8,128)(2,1)}, u32[]{:S(2)}, u32[]{:S(2)}) collective-permute-start(bf16[1024,1024]{1,0:T(8,128)(2,1)} %dense_weights.2), channel_id=1, source_target_pairs={{0,16},{16,0},{1,17},{17,1},{2,18},{18,2},{3,19},{19,3},{4,20},{20... | collective-permute-start | bytes 6291464 | tf_op jit(solution)/shard_map/ppermute | solution.py:44
  24.8 15.0 %collective-permute-start.5 = (bf16[4,32,2048]{2,1,0:T(8,128)(2,1)S(1)}, bf16[4,32,2048]{2,1,0:T(8,128)(2,1)S(1)}, u32[]{:S(2)}, u32[]{:S(2)}) collective-permute-start(bf16[4,32,2048]{2,1,0:T(8,128)(2,1)S(1)} %fusion.19.refs_2_), channel_id=1, source_target_pairs={{0,2},{1,3},{2,0},{3,1},{4,6},{5,7},{6,4},{7,5},{8,10},{9,11},{10,... | collective-permute-start | bytes 1572872 | tf_op jit(solution)/shard_map/ppermute | solution.py:22
  49.5 65.5 %collective-permute-start.17 = (bf16[1024,1024]{1,0:T(8,128)(2,1)}, bf16[1024,1024]{1,0:T(8,128)(2,1)}, u32[]{:S(2)}, u32[]{:S(2)}) collective-permute-start(bf16[1024,1024]{1,0:T(8,128)(2,1)} %dense_weights.3), channel_id=1, source_target_pairs={{0,16},{16,0},{1,17},{17,1},{2,18},{18,2},{3,19},{19,3},{4,20},{20... | collective-permute-start | bytes 6291464 | tf_op jit(solution)/shard_map/ppermute | solution.py:44
  49.5 25.3 %all-to-all-start.1 = ((bf16[4,128,1024]{2,1,0:T(8,128)(2,1)}), bf16[4,128,1024]{2,1,0:T(8,128)(2,1)S(1)}, u32[]{:S(2)}, u32[]{:S(2)}) async-start(bf16[4,128,1024]{2,1,0:T(8,128)(2,1)} %bitcast.179), calls=%async_computation.1 | async-start | bytes 2097152 | tf_op jit(solution)/shard_map/all_to_all | solution.py:36
  54.6 15.2 %collective-permute-start.12 = (bf16[4,32,2048]{2,1,0:T(8,128)(2,1)S(1)}, bf16[4,32,2048]{2,1,0:T(8,128)(2,1)S(1)}, u32[]{:S(2)}, u32[]{:S(2)}) collective-permute-start(bf16[4,32,2048]{2,1,0:T(8,128)(2,1)S(1)} %fusion.23.refs_6_), channel_id=1, source_target_pairs={{0,1},{1,2},{2,3},{3,0},{4,5},{5,6},{6,7},{7,4},{8,9},{9,10},{10,1... | collective-permute-start | bytes 1572872 | tf_op jit(solution)/shard_map/ppermute | solution.py:22
  54.6 15.1 %collective-permute-start.11 = (bf16[4,32,2048]{2,1,0:T(8,128)(2,1)S(1)}, bf16[4,32,2048]{2,1,0:T(8,128)(2,1)S(1)}, u32[]{:S(2)}, u32[]{:S(2)}) collective-permute-start(bf16[4,32,2048]{2,1,0:T(8,128)(2,1)S(1)} %fusion.23.refs_6_), channel_id=1, source_target_pairs={{0,2},{1,3},{2,0},{3,1},{4,6},{5,7},{6,4},{7,5},{8,10},{9,11},{10,... | collective-permute-start | bytes 1572872 | tf_op jit(solution)/shard_map/ppermute | solution.py:22
  56.5 14.0 %collective-permute-start.10 = (bf16[4,32,2048]{2,1,0:T(8,128)(2,1)S(1)}, bf16[4,32,2048]{2,1,0:T(8,128)(2,1)S(1)}, u32[]{:S(2)}, u32[]{:S(2)}) collective-permute-start(bf16[4,32,2048]{2,1,0:T(8,128)(2,1)S(1)} %fusion.23.refs_6_), channel_id=1, source_target_pairs={{0,3},{1,0},{2,1},{3,2},{4,7},{5,4},{6,5},{7,6},{8,11},{9,8},{10,9... | collective-permute-start | bytes 1572872 | tf_op jit(solution)/shard_map/ppermute | solution.py:22
  72.9 15.7 %collective-permute-start.13 = (bf16[4,4,32,1024]{3,2,1,0:T(8,128)(2,1)}, bf16[4,4,32,1024]{3,2,1,0:T(8,128)(2,1)}, u32[]{:S(2)}, u32[]{:S(2)}) collective-permute-start(bf16[4,4,32,1024]{3,2,1,0:T(8,128)(2,1)} %slice.238), channel_id=1, source_target_pairs={{0,16},{16,0},{1,17},{17,1},{2,18},{18,2},{3,19},{19,3},{4,20},{20... | collective-permute-start | bytes 3145736 | tf_op jit(solution)/shard_map/ppermute | solution.py:44
  77.1 15.7 %collective-permute-start.22 = (bf16[4,128,1024]{2,1,0:T(8,128)(2,1)}, bf16[4,128,1024]{2,1,0:T(8,128)(2,1)}, u32[]{:S(2)}, u32[]{:S(2)}) collective-permute-start(bf16[4,128,1024]{2,1,0:T(8,128)(2,1)} %in_turn.1), channel_id=1, source_target_pairs={{0,3},{1,0},{2,1},{3,2},{4,7},{5,4},{6,5},{7,6},{8,11},{9,8},{10,9... | collective-permute-start | bytes 3145736 | tf_op jit(solution)/shard_map/ppermute | solution.py:22
  77.5 27.4 %all-to-all-start.2 = ((bf16[4,128,1024]{2,1,0:T(8,128)(2,1)}), bf16[4,128,1024]{2,1,0:T(8,128)(2,1)}, u32[]{:S(2)}, u32[]{:S(2)}) async-start(bf16[4,128,1024]{2,1,0:T(8,128)(2,1)} %broadcast_in_dim.86.refs_1_), calls=%async_computation.2 | async-start | bytes 2097152 | tf_op jit(solution)/shard_map/all_to_all | solution.py:36
  82.0 22.9 %collective-permute-start.23 = (bf16[4,128,1024]{2,1,0:T(8,128)(2,1)S(1)}, bf16[4,128,1024]{2,1,0:T(8,128)(2,1)}, u32[]{:S(2)}, u32[]{:S(2)}) collective-permute-start(bf16[4,128,1024]{2,1,0:T(8,128)(2,1)S(1)} %copy-done.1), channel_id=1, source_target_pairs={{0,1},{1,2},{2,3},{3,0},{4,5},{5,6},{6,7},{7,4},{8,9},{9,10},{10,1... | collective-permute-start | bytes 3145736 | tf_op jit(solution)/shard_map/ppermute | solution.py:22
  89.4 17.0 %collective-permute-start.16 = (bf16[128,1024]{1,0:T(8,128)(2,1)}, bf16[128,1024]{1,0:T(8,128)(2,1)}, u32[]{:S(2)}, u32[]{:S(2)}) collective-permute-start(bf16[128,1024]{1,0:T(8,128)(2,1)} %get-tuple-element.84), channel_id=1, source_target_pairs={{0,96},{32,0},{64,32},{96,64},{1,97},{33,1},{65,33},{97,65},{2,98}... | collective-permute-start | bytes 786440 | tf_op jit(solution)/shard_map/ppermute | solution.py:319
  92.3 14.1 %collective-permute-start.15 = (bf16[128,1024]{1,0:T(8,128)(2,1)}, bf16[128,1024]{1,0:T(8,128)(2,1)}, u32[]{:S(2)}, u32[]{:S(2)}) collective-permute-start(bf16[128,1024]{1,0:T(8,128)(2,1)} %get-tuple-element.85), channel_id=1, source_target_pairs={{0,64},{32,96},{64,0},{96,32},{1,65},{33,97},{65,1},{97,33},{2,66}... | collective-permute-start | bytes 786440 | tf_op jit(solution)/shard_map/ppermute | solution.py:319
  92.9 16.1 %collective-permute-start.14 = (bf16[128,1024]{1,0:T(8,128)(2,1)}, bf16[128,1024]{1,0:T(8,128)(2,1)}, u32[]{:S(2)}, u32[]{:S(2)}) collective-permute-start(bf16[128,1024]{1,0:T(8,128)(2,1)} %get-tuple-element.83), channel_id=1, source_target_pairs={{0,32},{32,64},{64,96},{96,0},{1,33},{33,65},{65,97},{97,1},{2,34}... | collective-permute-start | bytes 786440 | tf_op jit(solution)/shard_map/ppermute | solution.py:319
  104.9 23.6 %collective-permute-start.21 = (bf16[4,4,32,1024]{3,2,1,0:T(8,128)(2,1)}, bf16[4,4,32,1024]{3,2,1,0:T(8,128)(2,1)S(1)}, u32[]{:S(2)}, u32[]{:S(2)}) collective-permute-start(bf16[4,4,32,1024]{3,2,1,0:T(8,128)(2,1)} %bitcast.62.refs_4_), channel_id=1, source_target_pairs={{0,16},{16,0},{1,17},{17,1},{2,18},{18,2},{3,19},{19,3},{4,20},{20... | collective-permute-start | bytes 3145736 | tf_op jit(solution)/shard_map/ppermute | solution.py:44
  106.4 22.1 %collective-permute-start.24 = (bf16[4,128,1024]{2,1,0:T(8,128)(2,1)S(1)}, bf16[4,128,1024]{2,1,0:T(8,128)(2,1)}, u32[]{:S(2)}, u32[]{:S(2)}) collective-permute-start(bf16[4,128,1024]{2,1,0:T(8,128)(2,1)S(1)} %copy-done.1), channel_id=1, source_target_pairs={{0,2},{1,3},{2,0},{3,1},{4,6},{5,7},{6,4},{7,5},{8,10},{9,11},{10,... | collective-permute-start | bytes 3145736 | tf_op jit(solution)/shard_map/ppermute | solution.py:22
  111.5 17.0 %all-to-all-start.3 = ((bf16[4,128,1024]{2,1,0:T(8,128)(2,1)}), bf16[4,128,1024]{2,1,0:T(8,128)(2,1)S(1)}, u32[]{:S(2)}, u32[]{:S(2)}) async-start(bf16[4,128,1024]{2,1,0:T(8,128)(2,1)} %broadcast_in_dim.91), calls=%async_computation.3 | async-start | bytes 2097152 | tf_op jit(solution)/shard_map/all_to_all | solution.py:36
  121.4 15.2 %collective-permute-start.20 = (bf16[4,32,2048]{2,1,0:T(8,128)(2,1)}, bf16[4,32,2048]{2,1,0:T(8,128)(2,1)}, u32[]{:S(2)}, u32[]{:S(2)}) collective-permute-start(bf16[4,32,2048]{2,1,0:T(8,128)(2,1)} %bitcast.60), channel_id=1, source_target_pairs={{0,3},{1,0},{2,1},{3,2},{4,7},{5,4},{6,5},{7,6},{8,11},{9,8},{10,9... | collective-permute-start | bytes 1572872 | tf_op jit(solution)/shard_map/ppermute | solution.py:22
  122.0 16.9 %collective-permute-start.19 = (bf16[4,32,2048]{2,1,0:T(8,128)(2,1)}, bf16[4,32,2048]{2,1,0:T(8,128)(2,1)}, u32[]{:S(2)}, u32[]{:S(2)}) collective-permute-start(bf16[4,32,2048]{2,1,0:T(8,128)(2,1)} %bitcast.59), channel_id=1, source_target_pairs={{0,2},{1,3},{2,0},{3,1},{4,6},{5,7},{6,4},{7,5},{8,10},{9,11},{10,... | collective-permute-start | bytes 1572872 | tf_op jit(solution)/shard_map/ppermute | solution.py:22
  124.3 14.6 %collective-permute-start.18 = (bf16[4,32,2048]{2,1,0:T(8,128)(2,1)}, bf16[4,32,2048]{2,1,0:T(8,128)(2,1)}, u32[]{:S(2)}, u32[]{:S(2)}) collective-permute-start(bf16[4,32,2048]{2,1,0:T(8,128)(2,1)} %bitcast.58), channel_id=1, source_target_pairs={{0,1},{1,2},{2,3},{3,0},{4,5},{5,6},{6,7},{7,4},{8,9},{9,10},{10,1... | collective-permute-start | bytes 1572872 | tf_op jit(solution)/shard_map/ppermute | solution.py:22
  135.9 13.9 %collective-permute-start.28 = (bf16[4,32,2048]{2,1,0:T(8,128)(2,1)S(1)}, bf16[4,32,2048]{2,1,0:T(8,128)(2,1)S(1)}, u32[]{:S(2)}, u32[]{:S(2)}) collective-permute-start(bf16[4,32,2048]{2,1,0:T(8,128)(2,1)S(1)} %bitcast.182), channel_id=1, source_target_pairs={{0,3},{1,0},{2,1},{3,2},{4,7},{5,4},{6,5},{7,6},{8,11},{9,8},{10,9... | collective-permute-start | bytes 1572872 | tf_op jit(solution)/shard_map/ppermute | solution.py:22
  (34 other events, 206.5 us)

commit v3 on v2

--- a/solution.py
+++ b/solution.py
@@ -306,7 +306,7 @@
     slopes = silu_slope(h_mine)
     slopes = lax.optimization_barrier([slopes[:, :tk], slopes[:, tk:]])
 
-    other_a = swap(after(dy_a, h_other)[..., feats:])
+    other_a = swap(jnp.stack([after(piece, h_other)[..., feats:] for piece in pieces_a]))
     hg_a = hidden_grad(after(parts_a, other_a, *slopes), 0)
     line_b = after(line_b, h_other, *pieces_a)
     pieces_b = [line_b, *pieces_of(line_b)]

time: 174 us -> 173 us (level)
    unnamed x46 -> x44, local copies, waits for them, and re-layouts: 4.05 us -> 3.11 us
  transfers between devices with their start and end apart: 35 -> 35, of which waited for: 9 -> 9; matrix products, arithmetic and copies ran while one was open for 27% -> 27% of each run, Pallas kernels for 16% -> 17%
where the time goes in v3:
time: 173 us; the launch traced here: 171 us
  starting transfers between devices  61.9 us (36%)
  Pallas kernels  28.6 us (17%)
  waiting for transfers between devices  27.1 us (16%)
  local copies, waits for them, and re-layouts  22.6 us (13%)
  matrix products  19.7 us (11%)
  other arithmetic  10.4 us (6%)
    ppermute x18, starting transfers between devices, along(): return lax.ppermute(value, PLANE, pairs)  19.7 us
    dot_general x4, matrix products, dot(): lax.dot_general(a, b, (contract, ((), ())), preferred_element_type=jnp.fl...  19.7 us
    pallas_call x2, Pallas kernels, slot_grads(): pl.pallas_call(functools.partial(grads_kernel, down, len(lefts), len(owns...  19.5 us
    all_to_all x4, starting transfers between devices, exchange_z(): return lax.all_to_all(value, 'z', 0, 0, tiled=True)  18.1 us
    ppermute x9, starting transfers between devices, swap(): return lax.ppermute(value, 'c', [(0, 1), (1, 0)])  16.3 us
    all_to_all x1, waiting for transfers between devices, exchange_first(): lax.all_to_all(value, PLANE, 0, 0, axis_index_groups=lines, tiled=True)  9.74 us
    pallas_call x2, Pallas kernels, dense_weights(): pl.pallas_call(weights_kernel, grid_spec=pltpu.PrefetchScalarGridSpec(num...  9.06 us
    ppermute x18, waiting for transfers between devices, along(): return lax.ppermute(value, PLANE, pairs)  8.78 us
  transfers between devices with their start and end apart: 35, of which 9 were waited for; matrix products, arithmetic and copies ran while one was open for 27% of the time, Pallas kernels for 17%

profile of v3, /device:TPU:1, one launch (start us, length us, event | category | flops | bytes accessed | tf_op | source)
XLA Modules:
  0.0 171.5 jit_solution(1951291861404796099)
XLA Ops:
  5.0 2.9 %collective-permute-start.1 = (bf16[256,1024]{1,0:T(8,128)(2,1)S(1)}, bf16[256,1024]{1,0:T(8,128)(2,1)S(1)}, u32[]{:S(2)}, u32[]{:S(2)}) collective-permute-start(bf16[256,1024]{1,0:T(8,128)(2,1)S(1)} %pad_maximum_fusion.14), channel_id=1, source_target_pairs={{0,12},{1,13},{2,14},{3,15},{4,0},{5,1},{6,2},{7,3},{8,4},{9,5},{1... | collective-permute-start | bytes 1572872 | tf_op jit(solution)/shard_map/ppermute | solution.py:22
  10.5 5.0 %all-to-all-start = ((bf16[4,256,1024]{2,1,0:T(8,128)(2,1)}), bf16[4,256,1024]{2,1,0:T(8,128)(2,1)}, u32[]{:S(2)}, u32[]{:S(2)}) async-start(bf16[4,256,1024]{2,1,0:T(8,128)(2,1)} %broadcast_in_dim.84), calls=%async_computation | async-start | bytes 4194304 | tf_op jit(solution)/shard_map/all_to_all | solution.py:36
  15.5 5.1 %dense_weights.2 = bf16[1024,1024]{1,0:T(8,128)(2,1)} custom-call(s32[4]{0:T(128)} %bitcast.169, bf16[4,512,512]{2,1,0:T(8,128)(2,1)} %bitcast.177, bf16[4,512,512]{2,1,0:T(8,128)(2,1)} %bitcast.173), custom_call_target="tpu_custom_call" | custom-call | flops 2097152 | bytes 6291456 | tf_op jit(solution)/shard_map/dense_weights/pallas_call | solution.py:115
  24.8 2.5 %collective-permute-start.5 = (bf16[4,32,2048]{2,1,0:T(8,128)(2,1)S(1)}, bf16[4,32,2048]{2,1,0:T(8,128)(2,1)S(1)}, u32[]{:S(2)}, u32[]{:S(2)}) collective-permute-start(bf16[4,32,2048]{2,1,0:T(8,128)(2,1)S(1)} %fusion.19.refs_2_), channel_id=1, source_target_pairs={{0,2},{1,3},{2,0},{3,1},{4,6},{5,7},{6,4},{7,5},{8,10},{9,11},{10,... | collective-permute-start | bytes 1572872 | tf_op jit(solution)/shard_map/ppermute | solution.py:22
  29.6 4.0 %dense_weights.3 = bf16[1024,1024]{1,0:T(8,128)(2,1)} custom-call(s32[4]{0:T(128)} %bitcast.171, bf16[4,512,512]{2,1,0:T(8,128)(2,1)} %bitcast.178, bf16[4,512,512]{2,1,0:T(8,128)(2,1)} %bitcast.179), custom_call_target="tpu_custom_call" | custom-call | flops 2097152 | bytes 6291456 | tf_op jit(solution)/shard_map/dense_weights/pallas_call | solution.py:115
  35.5 4.3 %collective-permute-done.5.refs_4_ = bf16[4,32,2048]{2,1,0:T(8,128)(2,1)S(1)} collective-permute-done((bf16[4,32,2048]{2,1,0:T(8,128)(2,1)S(1)}, bf16[4,32,2048]{2,1,0:T(8,128)(2,1)S(1)}, u32[]{:S(2)}, u32[]{:S(2)}) %collective-permute-start.5) | collective-permute-done | bytes 524320 | tf_op jit(solution)/shard_map/ppermute | solution.py:22
  41.6 4.9 %fusion.2 = bf16[512,1024]{1,0:T(8,128)(2,1)} fusion(bf16[512,2048]{1,0:T(8,128)(2,1)S(1)} %bitcast.181, bf16[1024,1024]{1,0:T(8,128)(2,1)} %collective-permute-done.7, bf16[1024,1024]{1,0:T(8,128)(2,1)S(1)} %copy-done.11), kind=kOutput, calls=%fused_computation.8 | convolution fusion | flops 2156396544 | bytes 7340032 | tf_op jit(solution)/shard_map/dot_general | solution.py:234
  48.4 5.0 %all-to-all-start.1 = ((bf16[4,128,1024]{2,1,0:T(8,128)(2,1)}), bf16[4,128,1024]{2,1,0:T(8,128)(2,1)S(1)}, u32[]{:S(2)}, u32[]{:S(2)}) async-start(bf16[4,128,1024]{2,1,0:T(8,128)(2,1)} %bitcast.187), calls=%async_computation.1 | async-start | bytes 2097152 | tf_op jit(solution)/shard_map/all_to_all | solution.py:36
  61.0 3.3 %collective-permute-start.9 = (bf16[4,4,32,1024]{3,2,1,0:T(8,128)(2,1)}, bf16[4,4,32,1024]{3,2,1,0:T(8,128)(2,1)}, u32[]{:S(2)}, u32[]{:S(2)}) collective-permute-start(bf16[4,4,32,1024]{3,2,1,0:T(8,128)(2,1)} %pad_maximum_fusion.12), channel_id=1, source_target_pairs={{0,16},{16,0},{1,17},{17,1},{2,18},{18,2},{3,19},{19,3},{4,20},{20... | collective-permute-start | bytes 3145736 | tf_op jit(solution)/shard_map/ppermute | solution.py:44
  76.4 4.5 %all-to-all-start.2 = ((bf16[4,128,1024]{2,1,0:T(8,128)(2,1)}), bf16[4,128,1024]{2,1,0:T(8,128)(2,1)}, u32[]{:S(2)}, u32[]{:S(2)}) async-start(bf16[4,128,1024]{2,1,0:T(8,128)(2,1)} %broadcast_in_dim.86.refs_1_), calls=%async_computation.2 | async-start | bytes 2097152 | tf_op jit(solution)/shard_map/all_to_all | solution.py:36
  82.1 5.2 %fusion.3 = bf16[512,1024]{1,0:T(8,128)(2,1)S(1)} fusion(bf16[512,2048]{1,0:T(8,128)(2,1)} %bitcast.175, bf16[1024,1024]{1,0:T(8,128)(2,1)} %collective-permute-done.7, bf16[1024,1024]{1,0:T(8,128)(2,1)} %dense_weights.2), kind=kOutput, calls=%fused_computation.9 | convolution fusion | flops 2156396544 | bytes 7340032 | tf_op jit(solution)/shard_map/dot_general | solution.py:234
  88.3 2.9 %collective-permute-start.16 = (bf16[128,1024]{1,0:T(8,128)(2,1)}, bf16[128,1024]{1,0:T(8,128)(2,1)}, u32[]{:S(2)}, u32[]{:S(2)}) collective-permute-start(bf16[128,1024]{1,0:T(8,128)(2,1)} %get-tuple-element.90), channel_id=1, source_target_pairs={{0,96},{32,0},{64,32},{96,64},{1,97},{33,1},{65,33},{97,65},{2,98}... | collective-permute-start | bytes 786440 | tf_op jit(solution)/shard_map/ppermute | solution.py:319
  92.4 11.1 %slot_grads.2 = f32[4,512,512]{2,1,0:T(8,128)} custom-call(s32[4]{0:T(128)S(1)} %bitcast.170, s32[3]{0:T(128)S(1)} %add_convert_fusion.3.place_of, bf16[4,2,2,64,1024]{4,3,2,1,0:T(8,128)(2,1)} %bitcast.26.refs_0_, bf16[4,2,2,64,1024]{4,3,2,1,0:T(8,128)(2,1)} %collective-permute-done.8.refs_1_, bf16[4,32,2048]{2,1,0:T(8,128)(2,1)S(1)} %fusion.19.refs_2_, ...), custom_call_target="tpu_custom_call" | custom-call | flops 4294967296 | bytes 14680064 | tf_op jit(solution)/shard_map/slot_grads/pallas_call | solution.py:215
  105.8 2.0 %collective-permute-done.14 = bf16[128,1024]{1,0:T(8,128)(2,1)} collective-permute-done((bf16[128,1024]{1,0:T(8,128)(2,1)}, bf16[128,1024]{1,0:T(8,128)(2,1)}, u32[]{:S(2)}, u32[]{:S(2)}) %collective-permute-start.14) | collective-permute-done | bytes 262176 | tf_op jit(solution)/shard_map/ppermute | solution.py:319
  110.4 3.5 %all-to-all-start.3 = ((bf16[4,128,1024]{2,1,0:T(8,128)(2,1)}), bf16[4,128,1024]{2,1,0:T(8,128)(2,1)S(1)}, u32[]{:S(2)}, u32[]{:S(2)}) async-start(bf16[4,128,1024]{2,1,0:T(8,128)(2,1)} %broadcast_in_dim.91), calls=%async_computation.3 | async-start | bytes 2097152 | tf_op jit(solution)/shard_map/all_to_all | solution.py:36
  114.0 4.9 %convolution_convert_fusion.1 = bf16[512,2048]{1,0:T(8,128)(2,1)S(1)} fusion(bf16[512,1024]{1,0:T(8,128)(2,1)} %bitcast.60, bf16[1024,1024]{1,0:T(8,128)(2,1)} %collective-permute-done.17, bf16[1024,1024]{1,0:T(8,128)(2,1)} %dense_weights.3), kind=kOutput, calls=%fused_computation.3 | convolution fusion | flops 2156920832 | bytes 7340032 | tf_op jit(solution)/shard_map/dot_general | solution.py:234
  120.9 2.3 %collective-permute-start.19 = (bf16[4,32,2048]{2,1,0:T(8,128)(2,1)}, bf16[4,32,2048]{2,1,0:T(8,128)(2,1)}, u32[]{:S(2)}, u32[]{:S(2)}) collective-permute-start(bf16[4,32,2048]{2,1,0:T(8,128)(2,1)} %bitcast.63), channel_id=1, source_target_pairs={{0,2},{1,3},{2,0},{3,1},{4,6},{5,7},{6,4},{7,5},{8,10},{9,11},{10,... | collective-permute-start | bytes 1572872 | tf_op jit(solution)/shard_map/ppermute | solution.py:22
  123.2 5.6 %all-to-all-done.3 = bf16[4,128,1024]{2,1,0:T(8,128)(2,1)S(1)} async-done(((bf16[4,128,1024]{2,1,0:T(8,128)(2,1)}), bf16[4,128,1024]{2,1,0:T(8,128)(2,1)S(1)}, u32[]{:S(2)}, u32[]{:S(2)}) %all-to-all-start.3) | async-done | bytes 1048608 | tf_op jit(solution)/shard_map/all_to_all | solution.py:36
  130.0 4.6 %convolution_convert_fusion = bf16[512,2048]{1,0:T(8,128)(2,1)S(1)} fusion(bf16[512,1024]{1,0:T(8,128)(2,1)S(1)} %bitcast.167, bf16[1024,1024]{1,0:T(8,128)(2,1)} %collective-permute-done.17, bf16[1024,1024]{1,0:T(8,128)(2,1)} %dense_weights.3), kind=kOutput, calls=%fused_computation.2 | convolution fusion | flops 2156920832 | bytes 7340032 | tf_op jit(solution)/shard_map/dot_general | solution.py:234
  135.4 2.3 %collective-permute-start.27 = (bf16[4,32,2048]{2,1,0:T(8,128)(2,1)S(1)}, bf16[4,32,2048]{2,1,0:T(8,128)(2,1)S(1)}, u32[]{:S(2)}, u32[]{:S(2)}) collective-permute-start(bf16[4,32,2048]{2,1,0:T(8,128)(2,1)S(1)} %bitcast.189), channel_id=1, source_target_pairs={{0,2},{1,3},{2,0},{3,1},{4,6},{5,7},{6,4},{7,5},{8,10},{9,11},{10,... | collective-permute-start | bytes 1572872 | tf_op jit(solution)/shard_map/ppermute | solution.py:22
  140.5 8.5 %slot_grads.3 = f32[4,512,512]{2,1,0:T(8,128)} custom-call(s32[4]{0:T(128)S(1)} %bitcast.172, s32[3]{0:T(128)S(1)} %add_convert_fusion.3.place_of, bf16[4,2,64,1024]{3,2,1,0:T(8,128)(2,1)S(1)} %bitcast.160, bf16[4,2,64,1024]{3,2,1,0:T(8,128)(2,1)} %bitcast.73.refs_1_, bf16[4,2,64,1024]{3,2,1,0:T(8,128)(2,1)} %bitcast.74.refs_2_, ...), custom_call_target="tpu_custom_call" | custom-call | flops 4294967296 | bytes 14680064 | tf_op jit(solution)/shard_map/slot_grads/pallas_call | solution.py:215
  152.3 3.6 %all-to-all-start.4 = ((bf16[4,64,2048]{2,1,0:T(8,128)(2,1)}), bf16[4,64,2048]{2,1,0:T(8,128)(2,1)S(1)}, u32[]{:S(2)}, u32[]{:S(2)}) async-start(bf16[4,64,2048]{2,1,0:T(8,128)(2,1)} %pad_maximum_fusion.13), calls=%async_computation.4 | async-start | bytes 2097152 | tf_op jit(solution)/shard_map/all_to_all | solution.py:32
  156.0 9.7 %all-to-all-done.4 = bf16[4,64,2048]{2,1,0:T(8,128)(2,1)S(1)} async-done(((bf16[4,64,2048]{2,1,0:T(8,128)(2,1)}), bf16[4,64,2048]{2,1,0:T(8,128)(2,1)S(1)}, u32[]{:S(2)}, u32[]{:S(2)}) %all-to-all-start.4) | async-done | bytes 1048608 | tf_op jit(solution)/shard_map/all_to_all | solution.py:32
  165.9 3.9 %collective-permute-start.29 = (bf16[64,1024]{1,0:T(8,128)(2,1)S(1)}, bf16[64,1024]{1,0:T(8,128)(2,1)S(1)}, u32[]{:S(2)}, u32[]{:S(2)}) collective-permute-start(bf16[64,1024]{1,0:T(8,128)(2,1)S(1)} %slice.264), channel_id=1, source_target_pairs={{0,16},{16,0},{1,17},{17,1},{2,18},{18,2},{3,19},{19,3},{4,20},{20... | collective-permute-start | bytes 393224 | tf_op jit(solution)/shard_map/ppermute | solution.py:44
  (155 shorter events, 58.6 us)
Async XLA Ops:
  5.0 16.6 %collective-permute-start.1 = (bf16[256,1024]{1,0:T(8,128)(2,1)S(1)}, bf16[256,1024]{1,0:T(8,128)(2,1)S(1)}, u32[]{:S(2)}, u32[]{:S(2)}) collective-permute-start(bf16[256,1024]{1,0:T(8,128)(2,1)S(1)} %pad_maximum_fusion.14), channel_id=1, source_target_pairs={{0,12},{1,13},{2,14},{3,15},{4,0},{5,1},{6,2},{7,3},{8,4},{9,5},{1... | collective-permute-start | bytes 1572872 | tf_op jit(solution)/shard_map/ppermute | solution.py:22
  8.2 15.2 %collective-permute-start.3 = (bf16[256,1024]{1,0:T(8,128)(2,1)S(1)}, bf16[256,1024]{1,0:T(8,128)(2,1)S(1)}, u32[]{:S(2)}, u32[]{:S(2)}) collective-permute-start(bf16[256,1024]{1,0:T(8,128)(2,1)S(1)} %pad_maximum_fusion.14), channel_id=1, source_target_pairs={{0,4},{1,5},{2,6},{3,7},{4,8},{5,9},{6,10},{7,11},{8,12},{9,13},{1... | collective-permute-start | bytes 1572872 | tf_op jit(solution)/shard_map/ppermute | solution.py:22
  10.5 36.0 %all-to-all-start = ((bf16[4,256,1024]{2,1,0:T(8,128)(2,1)}), bf16[4,256,1024]{2,1,0:T(8,128)(2,1)}, u32[]{:S(2)}, u32[]{:S(2)}) async-start(bf16[4,256,1024]{2,1,0:T(8,128)(2,1)} %broadcast_in_dim.84), calls=%async_computation | async-start | bytes 4194304 | tf_op jit(solution)/shard_map/all_to_all | solution.py:36
  20.6 20.7 %collective-permute-start.7 = (bf16[1024,1024]{1,0:T(8,128)(2,1)}, bf16[1024,1024]{1,0:T(8,128)(2,1)}, u32[]{:S(2)}, u32[]{:S(2)}) collective-permute-start(bf16[1024,1024]{1,0:T(8,128)(2,1)} %dense_weights.2), channel_id=1, source_target_pairs={{0,16},{16,0},{1,17},{17,1},{2,18},{18,2},{3,19},{19,3},{4,20},{20... | collective-permute-start | bytes 6291464 | tf_op jit(solution)/shard_map/ppermute | solution.py:44
  24.8 15.0 %collective-permute-start.5 = (bf16[4,32,2048]{2,1,0:T(8,128)(2,1)S(1)}, bf16[4,32,2048]{2,1,0:T(8,128)(2,1)S(1)}, u32[]{:S(2)}, u32[]{:S(2)}) collective-permute-start(bf16[4,32,2048]{2,1,0:T(8,128)(2,1)S(1)} %fusion.19.refs_2_), channel_id=1, source_target_pairs={{0,2},{1,3},{2,0},{3,1},{4,6},{5,7},{6,4},{7,5},{8,10},{9,11},{10,... | collective-permute-start | bytes 1572872 | tf_op jit(solution)/shard_map/ppermute | solution.py:22
  48.4 65.5 %collective-permute-start.17 = (bf16[1024,1024]{1,0:T(8,128)(2,1)}, bf16[1024,1024]{1,0:T(8,128)(2,1)}, u32[]{:S(2)}, u32[]{:S(2)}) collective-permute-start(bf16[1024,1024]{1,0:T(8,128)(2,1)} %dense_weights.3), channel_id=1, source_target_pairs={{0,16},{16,0},{1,17},{17,1},{2,18},{18,2},{3,19},{19,3},{4,20},{20... | collective-permute-start | bytes 6291464 | tf_op jit(solution)/shard_map/ppermute | solution.py:44
  48.4 25.2 %all-to-all-start.1 = ((bf16[4,128,1024]{2,1,0:T(8,128)(2,1)}), bf16[4,128,1024]{2,1,0:T(8,128)(2,1)S(1)}, u32[]{:S(2)}, u32[]{:S(2)}) async-start(bf16[4,128,1024]{2,1,0:T(8,128)(2,1)} %bitcast.187), calls=%async_computation.1 | async-start | bytes 2097152 | tf_op jit(solution)/shard_map/all_to_all | solution.py:36
  53.5 15.2 %collective-permute-start.12 = (bf16[4,32,2048]{2,1,0:T(8,128)(2,1)S(1)}, bf16[4,32,2048]{2,1,0:T(8,128)(2,1)S(1)}, u32[]{:S(2)}, u32[]{:S(2)}) collective-permute-start(bf16[4,32,2048]{2,1,0:T(8,128)(2,1)S(1)} %fusion.23.refs_6_), channel_id=1, source_target_pairs={{0,1},{1,2},{2,3},{3,0},{4,5},{5,6},{6,7},{7,4},{8,9},{9,10},{10,1... | collective-permute-start | bytes 1572872 | tf_op jit(solution)/shard_map/ppermute | solution.py:22
  53.5 15.2 %collective-permute-start.11 = (bf16[4,32,2048]{2,1,0:T(8,128)(2,1)S(1)}, bf16[4,32,2048]{2,1,0:T(8,128)(2,1)S(1)}, u32[]{:S(2)}, u32[]{:S(2)}) collective-permute-start(bf16[4,32,2048]{2,1,0:T(8,128)(2,1)S(1)} %fusion.23.refs_6_), channel_id=1, source_target_pairs={{0,2},{1,3},{2,0},{3,1},{4,6},{5,7},{6,4},{7,5},{8,10},{9,11},{10,... | collective-permute-start | bytes 1572872 | tf_op jit(solution)/shard_map/ppermute | solution.py:22
  55.3 14.0 %collective-permute-start.10 = (bf16[4,32,2048]{2,1,0:T(8,128)(2,1)S(1)}, bf16[4,32,2048]{2,1,0:T(8,128)(2,1)S(1)}, u32[]{:S(2)}, u32[]{:S(2)}) collective-permute-start(bf16[4,32,2048]{2,1,0:T(8,128)(2,1)S(1)} %fusion.23.refs_6_), channel_id=1, source_target_pairs={{0,3},{1,0},{2,1},{3,2},{4,7},{5,4},{6,5},{7,6},{8,11},{9,8},{10,9... | collective-permute-start | bytes 1572872 | tf_op jit(solution)/shard_map/ppermute | solution.py:22
  71.7 15.6 %collective-permute-start.13 = (bf16[4,4,32,1024]{3,2,1,0:T(8,128)(2,1)}, bf16[4,4,32,1024]{3,2,1,0:T(8,128)(2,1)}, u32[]{:S(2)}, u32[]{:S(2)}) collective-permute-start(bf16[4,4,32,1024]{3,2,1,0:T(8,128)(2,1)} %slice.250), channel_id=1, source_target_pairs={{0,16},{16,0},{1,17},{17,1},{2,18},{18,2},{3,19},{19,3},{4,20},{20... | collective-permute-start | bytes 3145736 | tf_op jit(solution)/shard_map/ppermute | solution.py:44
  76.0 15.8 %collective-permute-start.22 = (bf16[4,128,1024]{2,1,0:T(8,128)(2,1)}, bf16[4,128,1024]{2,1,0:T(8,128)(2,1)}, u32[]{:S(2)}, u32[]{:S(2)}) collective-permute-start(bf16[4,128,1024]{2,1,0:T(8,128)(2,1)} %in_turn.1), channel_id=1, source_target_pairs={{0,3},{1,0},{2,1},{3,2},{4,7},{5,4},{6,5},{7,6},{8,11},{9,8},{10,9... | collective-permute-start | bytes 3145736 | tf_op jit(solution)/shard_map/ppermute | solution.py:22
  76.4 27.1 %all-to-all-start.2 = ((bf16[4,128,1024]{2,1,0:T(8,128)(2,1)}), bf16[4,128,1024]{2,1,0:T(8,128)(2,1)}, u32[]{:S(2)}, u32[]{:S(2)}) async-start(bf16[4,128,1024]{2,1,0:T(8,128)(2,1)} %broadcast_in_dim.86.refs_1_), calls=%async_computation.2 | async-start | bytes 2097152 | tf_op jit(solution)/shard_map/all_to_all | solution.py:36
  80.9 22.6 %collective-permute-start.23 = (bf16[4,128,1024]{2,1,0:T(8,128)(2,1)S(1)}, bf16[4,128,1024]{2,1,0:T(8,128)(2,1)}, u32[]{:S(2)}, u32[]{:S(2)}) collective-permute-start(bf16[4,128,1024]{2,1,0:T(8,128)(2,1)S(1)} %copy-done.1), channel_id=1, source_target_pairs={{0,1},{1,2},{2,3},{3,0},{4,5},{5,6},{6,7},{7,4},{8,9},{9,10},{10,1... | collective-permute-start | bytes 3145736 | tf_op jit(solution)/shard_map/ppermute | solution.py:22
  88.3 17.0 %collective-permute-start.16 = (bf16[128,1024]{1,0:T(8,128)(2,1)}, bf16[128,1024]{1,0:T(8,128)(2,1)}, u32[]{:S(2)}, u32[]{:S(2)}) collective-permute-start(bf16[128,1024]{1,0:T(8,128)(2,1)} %get-tuple-element.90), channel_id=1, source_target_pairs={{0,96},{32,0},{64,32},{96,64},{1,97},{33,1},{65,33},{97,65},{2,98}... | collective-permute-start | bytes 786440 | tf_op jit(solution)/shard_map/ppermute | solution.py:319
  91.2 14.6 %collective-permute-start.15 = (bf16[128,1024]{1,0:T(8,128)(2,1)}, bf16[128,1024]{1,0:T(8,128)(2,1)}, u32[]{:S(2)}, u32[]{:S(2)}) collective-permute-start(bf16[128,1024]{1,0:T(8,128)(2,1)} %get-tuple-element.91), channel_id=1, source_target_pairs={{0,64},{32,96},{64,0},{96,32},{1,65},{33,97},{65,1},{97,33},{2,66}... | collective-permute-start | bytes 786440 | tf_op jit(solution)/shard_map/ppermute | solution.py:319
  91.8 16.1 %collective-permute-start.14 = (bf16[128,1024]{1,0:T(8,128)(2,1)}, bf16[128,1024]{1,0:T(8,128)(2,1)}, u32[]{:S(2)}, u32[]{:S(2)}) collective-permute-start(bf16[128,1024]{1,0:T(8,128)(2,1)} %get-tuple-element.89), channel_id=1, source_target_pairs={{0,32},{32,64},{64,96},{96,0},{1,33},{33,65},{65,97},{97,1},{2,34}... | collective-permute-start | bytes 786440 | tf_op jit(solution)/shard_map/ppermute | solution.py:319
  103.5 25.3 %collective-permute-start.21 = (bf16[4,4,32,1024]{3,2,1,0:T(8,128)(2,1)}, bf16[4,4,32,1024]{3,2,1,0:T(8,128)(2,1)}, u32[]{:S(2)}, u32[]{:S(2)}) collective-permute-start(bf16[4,4,32,1024]{3,2,1,0:T(8,128)(2,1)} %bitcast.66.refs_4_), channel_id=1, source_target_pairs={{0,16},{16,0},{1,17},{17,1},{2,18},{18,2},{3,19},{19,3},{4,20},{20... | collective-permute-start | bytes 3145736 | tf_op jit(solution)/shard_map/ppermute | solution.py:44
  105.3 23.5 %collective-permute-start.24 = (bf16[4,128,1024]{2,1,0:T(8,128)(2,1)S(1)}, bf16[4,128,1024]{2,1,0:T(8,128)(2,1)}, u32[]{:S(2)}, u32[]{:S(2)}) collective-permute-start(bf16[4,128,1024]{2,1,0:T(8,128)(2,1)S(1)} %copy-done.1), channel_id=1, source_target_pairs={{0,2},{1,3},{2,0},{3,1},{4,6},{5,7},{6,4},{7,5},{8,10},{9,11},{10,... | collective-permute-start | bytes 3145736 | tf_op jit(solution)/shard_map/ppermute | solution.py:22
  110.4 18.4 %all-to-all-start.3 = ((bf16[4,128,1024]{2,1,0:T(8,128)(2,1)}), bf16[4,128,1024]{2,1,0:T(8,128)(2,1)S(1)}, u32[]{:S(2)}, u32[]{:S(2)}) async-start(bf16[4,128,1024]{2,1,0:T(8,128)(2,1)} %broadcast_in_dim.91), calls=%async_computation.3 | async-start | bytes 2097152 | tf_op jit(solution)/shard_map/all_to_all | solution.py:36
  120.3 15.1 %collective-permute-start.20 = (bf16[4,32,2048]{2,1,0:T(8,128)(2,1)}, bf16[4,32,2048]{2,1,0:T(8,128)(2,1)S(1)}, u32[]{:S(2)}, u32[]{:S(2)}) collective-permute-start(bf16[4,32,2048]{2,1,0:T(8,128)(2,1)} %bitcast.64), channel_id=1, source_target_pairs={{0,3},{1,0},{2,1},{3,2},{4,7},{5,4},{6,5},{7,6},{8,11},{9,8},{10,9... | collective-permute-start | bytes 1572872 | tf_op jit(solution)/shard_map/ppermute | solution.py:22
  120.9 16.8 %collective-permute-start.19 = (bf16[4,32,2048]{2,1,0:T(8,128)(2,1)}, bf16[4,32,2048]{2,1,0:T(8,128)(2,1)}, u32[]{:S(2)}, u32[]{:S(2)}) collective-permute-start(bf16[4,32,2048]{2,1,0:T(8,128)(2,1)} %bitcast.63), channel_id=1, source_target_pairs={{0,2},{1,3},{2,0},{3,1},{4,6},{5,7},{6,4},{7,5},{8,10},{9,11},{10,... | collective-permute-start | bytes 1572872 | tf_op jit(solution)/shard_map/ppermute | solution.py:22
  123.2 14.5 %collective-permute-start.18 = (bf16[4,32,2048]{2,1,0:T(8,128)(2,1)}, bf16[4,32,2048]{2,1,0:T(8,128)(2,1)}, u32[]{:S(2)}, u32[]{:S(2)}) collective-permute-start(bf16[4,32,2048]{2,1,0:T(8,128)(2,1)} %bitcast.62), channel_id=1, source_target_pairs={{0,1},{1,2},{2,3},{3,0},{4,5},{5,6},{6,7},{7,4},{8,9},{9,10},{10,1... | collective-permute-start | bytes 1572872 | tf_op jit(solution)/shard_map/ppermute | solution.py:22
  134.7 14.2 %collective-permute-start.28 = (bf16[4,32,2048]{2,1,0:T(8,128)(2,1)S(1)}, bf16[4,32,2048]{2,1,0:T(8,128)(2,1)S(1)}, u32[]{:S(2)}, u32[]{:S(2)}) collective-permute-start(bf16[4,32,2048]{2,1,0:T(8,128)(2,1)S(1)} %bitcast.190), channel_id=1, source_target_pairs={{0,3},{1,0},{2,1},{3,2},{4,7},{5,4},{6,5},{7,6},{8,11},{9,8},{10,9... | collective-permute-start | bytes 1572872 | tf_op jit(solution)/shard_map/ppermute | solution.py:22
  (33 other events, 199.3 us)
